TPU v7x, 128 devices: a whole 4x4x4 slice. The times are simulated.
128 devices in a mesh: gx: 8 (over x, core), gy: 16 (over z, y).
Axes of the slice: x: 4, y: 4, z: 4, core: 2. Of those that a mesh axis runs over, the one named last changes fastest.
Arguments:
- rock_type: int32 [128, 512, 512], P('gx', 'gy'), may hold values from 0 to 7
- rock_perm: float32 [8], replicated, may hold values from 0.05 to 0.5
- rock_poro: float32 [8], replicated, may hold values from 0.1 to 0.35
- base_flux: float32 [128, 512, 512], P('gx', 'gy'), may hold values from 0.5 to 2
- initial_pressure: float32 [128, 512, 512], P('gx', 'gy'), may hold values from -6 to 6
- old_saturation: float32 [128, 512, 512], P('gx', 'gy'), may hold values from 0 to 1
- well_cells: int32 [3, 512], replicated, may hold values from 0 to 511, as said below
- well_rates: float32 [512], replicated, may hold values from -2 to 2
Outputs:
- pressure: float32 [128, 512, 512], P('gx', 'gy')
- saturation: float32 [128, 512, 512], P('gx', 'gy')
Inputs may be any that keep to these rules, and one draw needn't show every extreme that they name: `well_cells`: row 0 holds first coordinates below 128, row 1 second coordinates below 512, row 2 third coordinates below 512. The first well lies in the last cell of the grid and the second in the first cell; wells may share a cell.
All inputs are finite; a program needn't handle non-finite values.
Results may differ from a plain program's by a relative error of at most 0.0003.
Values sent between devices are 32-bit elements; how exact they have to be, the bound alone decides.
A program may use at most 64 MiB of HBM per device.

v0:
```python
import jax
import jax.numpy as jnp
from jax import lax
from jax.sharding import PartitionSpec as P

PASSES = 4
NEWTON = 3


MOBILITY = 0.5
OMEGA = 0.8
VOLUME = 4.0
COMPRESS = 0.5


def padded(block, sides, width):
    for axis, dim in sides:
        count = lax.axis_size(axis)
        forward = [(i, i + 1) for i in range(count - 1)]
        backward = [(target, source) for source, target in forward]
        low = lax.ppermute(
            lax.slice_in_dim(block, block.shape[dim] - width, None, axis=dim), axis, forward
        )
        high = lax.ppermute(lax.slice_in_dim(block, 0, width, axis=dim), axis, backward)
        block = jnp.concatenate([low, block, high], axis=dim)
    return block


def passed_along(value, axis, by):
    length = lax.axis_size(axis)
    pairs = [(i, i + by) for i in range(length) if 0 <= i + by < length]
    return lax.ppermute(value, axis, pairs)


def fraction(water):
    denom = water * water + MOBILITY * (1.0 - water) ** 2
    return water * water / denom


def fraction_slope(water):
    denom = water * water + MOBILITY * (1.0 - water) ** 2
    return 2.0 * MOBILITY * water * (1.0 - water) / (denom * denom)


def transmit(left, right):
    total = left + right
    return 2.0 * left * right / jnp.where(total > 0, total, 1.0)


def along_depth(field):
    deeper = jnp.pad(field[:, :, 1:], ((0, 0), (0, 0), (0, 1)))
    shallower = jnp.pad(field[:, :, :-1], ((0, 0), (0, 0), (1, 0)))
    return (deeper, shallower)


def links(perm_ext):
    center = perm_ext[1:-1, 1:-1]
    deeper, shallower = along_depth(center)
    return (
        transmit(center, perm_ext[2:, 1:-1]),
        transmit(center, perm_ext[:-2, 1:-1]),
        transmit(center, perm_ext[1:-1, 2:]),
        transmit(center, perm_ext[1:-1, :-2]),
        transmit(center, deeper),
        transmit(center, shallower),
    )


def jacobi(press_ext, perm_ext, storage, source):
    east, west, north, south, below, above = links(perm_ext)
    center = press_ext[1:-1, 1:-1]
    deeper, shallower = along_depth(center)
    flow = (
        east * (center - press_ext[2:, 1:-1])
        + west * (center - press_ext[:-2, 1:-1])
        + north * (center - press_ext[1:-1, 2:])
        + south * (center - press_ext[1:-1, :-2])
        + below * (center - deeper)
        + above * (center - shallower)
    )
    outside = jnp.where(perm_ext[1:-1, 1:-1] > 0, 0.0, 1.0)
    diagonal = storage + east + west + north + south + below + above + outside
    return center + OMEGA * (source - storage * center - flow) / diagonal


def upwind(flux, own, other):
    return jnp.maximum(flux, 0.0) * own + jnp.minimum(flux, 0.0) * other


def water_terms(press_ext, perm_ext, frac_old, frac_side, base_flux, rates_field):
    east, west, north, south, below, above = links(perm_ext)
    center = press_ext[1:-1, 1:-1]
    deeper, shallower = along_depth(center)
    frac_deep, frac_shallow = along_depth(frac_old)
    through = jnp.maximum(base_flux + east * (center - press_ext[2:, 1:-1]), 0.0)
    leaving = (
        upwind(north * (center - press_ext[1:-1, 2:]), frac_old, frac_side[:, 2:])
        + upwind(south * (center - press_ext[1:-1, :-2]), frac_old, frac_side[:, :-2])
        + upwind(below * (center - deeper), frac_old, frac_deep)
        + upwind(above * (center - shallower), frac_old, frac_shallow)
    )
    explicit = jnp.maximum(rates_field, 0.0) + jnp.minimum(rates_field, 0.0) * frac_old - leaving
    return (through, explicit)


def sweep(inflow, volume, through, explicit, old_sat):

    def advance(incoming, items):
        vol_row, flux_row, extra_row, start_row = items
        water = start_row
        for _ in range(NEWTON):
            misfit = (
                vol_row * (water - start_row) + flux_row * fraction(water) - incoming - extra_row
            )
            water = jnp.clip(
                water - misfit / (vol_row + flux_row * fraction_slope(water)), 0.0, 1.0
            )
        return (flux_row * fraction(water), water)

    outgoing, saturation = lax.scan(advance, inflow, (volume, through, explicit, old_sat))
    return (saturation, outgoing)


def lookup(rock_type, table):
    result = jnp.zeros(rock_type.shape, table.dtype)
    for kind in range(table.shape[0]):
        result = jnp.where(rock_type == kind, table[kind], result)
    return result


def well_field(well_cells, well_rates, shape, anchor_x, anchor_y):
    local_x = well_cells[0] - anchor_x
    local_y = well_cells[1] - anchor_y
    local_z = well_cells[2]
    inside = (
        (local_x >= 0)
        & (local_x < shape[0])
        & (local_y >= 0)
        & (local_y < shape[1])
        & (local_z >= 0)
        & (local_z < shape[2])
    )
    count = shape[0] * shape[1] * shape[2]
    flat = jnp.where(inside, (local_x * shape[1] + local_y) * shape[2] + local_z, count)
    return (
        jnp.zeros((count,), well_rates.dtype).at[flat].add(well_rates, mode="drop").reshape(shape)
    )


def shards(
    rock_type,
    rock_perm,
    rock_poro,
    base_flux,
    initial_pressure,
    old_saturation,
    well_cells,
    well_rates,
):
    shape = rock_type.shape
    rank_x = lax.axis_index("gx")
    anchor_x = rank_x * shape[0]
    anchor_y = lax.axis_index("gy") * shape[1]
    perm = lookup(rock_type, rock_perm)
    volume = VOLUME * lookup(rock_type, rock_poro)
    storage = COMPRESS * volume
    rates_field = well_field(well_cells, well_rates, shape, anchor_x, anchor_y)
    source = storage * initial_pressure + rates_field
    pressure = initial_pressure
    perm_ext = padded(perm, (("gx", 0), ("gy", 1)), 1)
    for _ in range(PASSES):
        press_ext = padded(pressure, (("gx", 0), ("gy", 1)), 1)
        pressure = jacobi(press_ext, perm_ext, storage, source)
    side_ext = padded(pressure, (("gy", 1),), 1)
    next_layer = passed_along(pressure[:1], "gx", -1)
    next_wide = jnp.pad(next_layer, ((0, 0), (1, 1), (0, 0)))
    press_ext = jnp.concatenate([jnp.zeros_like(next_wide), side_ext, next_wide], axis=0)
    frac_old = fraction(old_saturation)
    frac_side = padded(frac_old, (("gy", 1),), 1)
    through, explicit = water_terms(
        press_ext, perm_ext, frac_old, frac_side, base_flux, rates_field
    )
    inlet = base_flux[0]
    upstream_end = rank_x == 0

    def turn(step, carry):
        current, arriving, leaving_water = carry
        inflow = jnp.where(upstream_end, inlet, arriving)

        def compute(operands):
            return sweep(operands, volume, through, explicit, old_saturation)

        def keep(operands):
            return (current, leaving_water)

        current, leaving_water = lax.cond(step == rank_x, compute, keep, inflow)
        arriving = passed_along(leaving_water, "gx", 1)
        return (current, arriving, leaving_water)

    zeros_face = jnp.zeros_like(inlet)
    saturation, _, _ = lax.fori_loop(
        0, lax.axis_size("gx"), turn, (old_saturation, zeros_face, zeros_face)
    )
    return (pressure, saturation)


def solution(mesh):
    return jax.shard_map(
        shards,
        mesh=mesh,
        in_specs=(
            P("gx", "gy", None),
            P(),
            P(),
            P("gx", "gy", None),
            P("gx", "gy", None),
            P("gx", "gy", None),
            P(),
            P(),
        ),
        out_specs=(P("gx", "gy", None), P("gx", "gy", None)),
        check_vma=False,
    )
```

profile of v0, /device:TPU:103, one launch (start us, length us, event | category | flops | bytes accessed | tf_op | source)
XLA Modules:
  0.0 495.5 jit_solution(13230162043304086703)
XLA Ops:
  0.6 1.6 fusion.153
  2.3 1.6 fusion.152
  3.9 9.2 %broadcast_multiply_fusion = (f32[16,32,512]{2,1,0:T(8,128)}, f32[16,32,512]{2,1,0:T(8,128)}, pred[16,32,512]{2,1,0:T(8,128)(4,1)S(1)}, pred[16,32,512]{2,1,0:T(...) fusion(f32[]{:T(128)} %bitcast.12, f32[]{:T(128)} %bitcast.11, ...), kind=kLoop, calls=%fused_computation.209 | loop fusion | flops 4456448 | bytes 5242912 | tf_op jit(solution)/shard_map/mul | solution.py:165
  13.0 5.9 %select_select_fusion = f32[16,32,512]{2,1,0:T(8,128)S(1)} fusion(pred[16,32,512]{2,1,0:T(8,128)(4,1)S(1)} %get-tuple-element.305, pred[16,32,512]{2,1,0:T(8,128)(4,1)S(1)} %get-tuple-element.304, pred[16,32,512]{2,1,0:T(8,128)(4,1)S(1)} %get-tuple-element.303, pred[16,32,512]{2,1,0:T(8,128)(4,1)S(1)} %get-tuple-element.302, ...), kind=kLoop, calls=%fused_computation.205 | loop fusion | flops 2097152 | bytes 3145760 | tf_op jit(solution)/shard_map/jit(_where)/select_n | solution.py:127
  19.0 2.6 collective-permute-start.1
  24.8 4.4 collective-permute-start.2
  29.2 2.7 fusion.148
  33.8 4.5 collective-permute-start.5
  38.3 1.9 collective-permute-start.7
  42.8 5.5 %collective-permute-start.6 = (f32[18,1,512]{2,1,0:T(1,128)}, f32[18,1,512]{2,1,0:T(1,128)S(1)}, u32[]{:S(2)}, u32[]{:S(2)}) collective-permute-start(f32[18,1,512]{2,1,0:T(1,128)} %get-tuple-element.318), channel_id=1, source_target_pairs={{1,0},{2,1},{3,2},{4,3},{5,4},{6,5},{7,6},{8,7},{9,8},{10,9},{11,1... | collective-permute-start | bytes 110600 | tf_op jit(solution)/shard_map/ppermute | solution.py:24
  48.3 1.9 collective-permute-start.8
  50.3 4.5 scatter_custom_fusion
  54.8 1.4 reshape.122
  56.8 6.7 %fusion.114 = (f32[16,32,512]{2,1,0:T(8,128)S(1)}, f32[16,32,512]{2,1,0:T(8,128)S(1)}, f32[16,32,512]{2,1,0:T(8,128)S(1)}, pred[16,32,512]{2,1,0:T(8,128)(4,1)S(1)}) fusion(f32[16,32,512]{2,1,0:T(8,128)S(1)} %copy-done, f32[18,32,512]{2,1,0:T(8,128)} %copy-done.17, f32[18,1,512]{2,1,0:T(1,128)} %collective-permute-done.8, f32[18,1,512]{2,1,0:T(1,128)} %copy-done.25, ...), kind=kLoop, calls=%fused_computation.176 | loop fusion | flops 20185088 | bytes 13377536 | tf_op jit(solution)/shard_map/add | solution.py:83
  64.9 4.5 collective-permute-start.9
  70.1 5.7 %collective-permute-start.24 = (f32[16,1,512]{2,1,0:T(1,128)}, f32[16,1,512]{2,1,0:T(1,128)}, u32[]{:S(2)}, u32[]{:S(2)}) collective-permute-start(f32[16,1,512]{2,1,0:T(1,128)} %get-tuple-element.324), channel_id=1, source_target_pairs={{1,0},{2,1},{3,2},{4,3},{5,4},{6,5},{7,6},{8,7},{9,8},{10,9},{11,1... | collective-permute-start | bytes 98312 | tf_op jit(solution)/shard_map/ppermute | solution.py:24
  75.8 1.9 collective-permute-start.25
  77.8 5.5 %collective-permute-start.11 = (f32[18,1,512]{2,1,0:T(1,128)S(1)}, f32[18,1,512]{2,1,0:T(1,128)S(1)}, u32[]{:S(2)}, u32[]{:S(2)}) collective-permute-start(f32[18,1,512]{2,1,0:T(1,128)S(1)} %get-tuple-element.314), channel_id=1, source_target_pairs={{1,0},{2,1},{3,2},{4,3},{5,4},{6,5},{7,6},{8,7},{9,8},{10,9},{11,1... | collective-permute-start | bytes 110600 | tf_op jit(solution)/shard_map/ppermute | solution.py:24
  83.4 2.1 collective-permute-start.12
  85.8 4.5 collective-permute-done.12
  90.3 3.0 fusion.97
  93.3 5.6 %collective-permute-start.13 = (f32[1,32,512]{2,1,0:T(8,128)S(1)}, f32[1,32,512]{2,1,0:T(8,128)S(1)}, u32[]{:S(2)}, u32[]{:S(2)}) collective-permute-start(f32[1,32,512]{2,1,0:T(8,128)S(1)} %get-tuple-element.335), channel_id=1, source_target_pairs={{16,0},{32,16},{48,32},{64,48},{80,64},{96,80},{112,96},{17,1},{33... | collective-permute-start | bytes 196616 | tf_op jit(solution)/shard_map/ppermute | solution.py:24
  100.3 1.7 fusion.139
  102.2 1.9 collective-permute-start.15
  104.1 3.5 collective-permute-start.16
  108.1 2.9 collective-permute-done.16
  110.9 3.0 fusion.80
  115.6 6.1 %collective-permute-start.17 = (f32[1,32,512]{2,1,0:T(8,128)}, f32[1,32,512]{2,1,0:T(8,128)}, u32[]{:S(2)}, u32[]{:S(2)}) collective-permute-start(f32[1,32,512]{2,1,0:T(8,128)} %get-tuple-element.331), channel_id=1, source_target_pairs={{16,0},{32,16},{48,32},{64,48},{80,64},{96,80},{112,96},{17,1},{33... | collective-permute-start | bytes 196616 | tf_op jit(solution)/shard_map/ppermute | solution.py:24
  123.1 1.5 slice_bitcast_fusion
  126.7 1.9 collective-permute-start.19
  128.7 3.6 collective-permute-start.20
  132.7 3.0 collective-permute-done.20
  135.8 3.8 fusion.63
  139.7 1.9 collective-permute-start.21
  141.7 5.7 %collective-permute-start.22 = (f32[16,1,512]{2,1,0:T(1,128)S(1)}, f32[16,1,512]{2,1,0:T(1,128)S(1)}, u32[]{:S(2)}, u32[]{:S(2)}) collective-permute-start(f32[16,1,512]{2,1,0:T(1,128)S(1)} %get-tuple-element.327), channel_id=1, source_target_pairs={{1,0},{2,1},{3,2},{4,3},{5,4},{6,5},{7,6},{8,7},{9,8},{10,9},{11,1... | collective-permute-start | bytes 98312 | tf_op jit(solution)/shard_map/ppermute | solution.py:24
  147.8 5.1 %collective-permute-start.23 = (f32[1,32,512]{2,1,0:T(8,128)S(1)}, f32[1,32,512]{2,1,0:T(8,128)S(1)}, u32[]{:S(2)}, u32[]{:S(2)}) collective-permute-start(f32[1,32,512]{2,1,0:T(8,128)S(1)} %slice.403), channel_id=1, source_target_pairs={{16,0},{32,16},{48,32},{64,48},{80,64},{96,80},{112,96},{17,1},{33... | collective-permute-start | bytes 196616 | tf_op jit(solution)/shard_map/ppermute | solution.py:32
  153.0 5.1 %fusion.43 = f32[16,32,512]{2,1,0:T(8,128)} fusion(f32[16,32,512]{2,1,0:T(8,128)S(1)} %copy-done.11, f32[16,1,512]{2,1,0:T(1,128)} %collective-permute-done.25, f32[16,1,512]{2,1,0:T(1,128)} %collective-permute-done.24, f32[16,32,511]{2,1,0:T(8,128)S(1)} %copy-done.15, f32[16,32,512]{2,1,0:T(8,128)S(1)} %copy-done.7, f32[16,32,512]{2,1,0:T(8,128)S(1)} %fusion.63, ...), kind=kLoop, calls=%fused_computation.73 | loop fusion | flops 14942208 | bytes 11862016 | tf_op jit(solution)/shard_map/sub | solution.py:102
  159.2 336.3 %while.29 = (s32[]{:T(128)}, f32[16,32,512]{2,1,0:T(8,128)}, f32[32,512]{1,0:T(8,128)S(1)}, f32[32,512]{1,0:T(8,128)}, s32[]{:T(128)}, /*index=5*/pred[]{:T(512)...) while((s32[]{:T(128)}, f32[16,32,512]{2,1,0:T(8,128)}, ...), condition=%wide.region_6.7_spmd, body=%wide.region_1.6_spmd.sunk | while | flops 1114118 | bytes 1115053 | solution.py:201
  160.5 2.1 collective-permute-done
  163.8 4.0 collective-permute-done
  169.1 4.5 collective-permute-done
  174.9 4.5 collective-permute-done
  180.7 4.5 collective-permute-done
  186.5 4.5 collective-permute-done
  192.3 261.0 %collective-permute-done = f32[32,512]{1,0:T(8,128)S(1)} collective-permute-done((f32[32,512]{1,0:T(8,128)}, f32[32,512]{1,0:T(8,128)S(1)}, u32[]{:S(2)}, u32[]{:S(2)}) %collective-permute-start) | collective-permute-done | bytes 65568 | tf_op jit(solution)/shard_map/while/body/eval_jaxpr/ppermute | solution.py:32
  453.3 38.8 %conditional.2 = ((f32[16,32,512]{2,1,0:T(8,128)}, f32[32,512]{1,0:T(8,128)})) conditional(s32[]{:T(128)} %convert_element_type.34, (f32[16,32,512]{2,1,0:T(8,128)}, f32[32,512]{1,0:T(8,128)}) %tuple.101, (pred[]{:T(512)}, f32[32,512]{1,0:T(8,128)S(1)}, f32[32,512]{1,0:T(8,128)S(1)}, f32[16,32,512]{2,1,0:T(8,128)S(1)}, f32[16,32,512]{2,1,0:T(8,128)}, ...), branch_computations={%region_2.2_spmd, %region_3.5_spmd} | conditional | flops 1114114 | bytes 852666 | solution.py:196
  453.9 38.2 %while.28 = (s32[]{:T(128)}, f32[32,512]{1,0:T(8,128)}, f32[16,32,512]{2,1,0:T(8,128)}, f32[16,32,512]{2,1,0:T(8,128)S(1)}, f32[16,32,512]{2,1,0:T(8,128)}, /*in...) while((s32[]{:T(128)}, f32[32,512]{1,0:T(8,128)}, f32[16,32,512]{2,1,0:T(8,128)}, ...), condition=%wide.region_5.4_spmd, body=%wide.region_4.3_spmd.sunk | while | flops 1097730 | bytes 655961 | solution.py:120
  453.9 1.7 bitcast_dynamic-update-slice_fusion.2
  456.3 1.7 bitcast_dynamic-update-slice_fusion.2
  458.7 1.7 bitcast_dynamic-update-slice_fusion.2
  461.1 1.7 bitcast_dynamic-update-slice_fusion.2
  463.5 1.7 bitcast_dynamic-update-slice_fusion.2
  465.9 1.7 bitcast_dynamic-update-slice_fusion.2
  468.2 1.7 bitcast_dynamic-update-slice_fusion.2
  470.6 1.7 bitcast_dynamic-update-slice_fusion.2
  473.0 1.7 bitcast_dynamic-update-slice_fusion.2
  475.4 1.7 bitcast_dynamic-update-slice_fusion.2
  477.8 1.7 bitcast_dynamic-update-slice_fusion.2
  480.2 1.7 bitcast_dynamic-update-slice_fusion.2
  482.6 1.7 bitcast_dynamic-update-slice_fusion.2
  485.0 1.7 bitcast_dynamic-update-slice_fusion.2
  487.3 1.7 bitcast_dynamic-update-slice_fusion.2
  489.7 1.7 bitcast_dynamic-update-slice_fusion.2
  493.4 2.1 collective-permute-done
  (140 shorter events, 41.1 us)
Async XLA Ops:
  13.0 9.8 %copy-start = (f32[16,32,512]{2,1,0:T(8,128)S(1)}, f32[16,32,512]{2,1,0:T(8,128)}, u32[]{:S(2)}) copy-start(f32[16,32,512]{2,1,0:T(8,128)} %param.18) | copy-start | bytes 3145732
  19.0 14.2 %collective-permute-start.1 = (f32[1,32,512]{2,1,0:T(8,128)S(1)}, f32[1,32,512]{2,1,0:T(8,128)S(1)}, u32[]{:S(2)}, u32[]{:S(2)}) collective-permute-start(f32[1,32,512]{2,1,0:T(8,128)S(1)} %get-tuple-element.342), channel_id=1, source_target_pairs={{16,0},{32,16},{48,32},{64,48},{80,64},{96,80},{112,96},{17,1},{33... | collective-permute-start | bytes 196616 | tf_op jit(solution)/shard_map/ppermute | solution.py:24
  21.6 11.6 %collective-permute-start.3 = (f32[1,32,512]{2,1,0:T(8,128)S(1)}, f32[1,32,512]{2,1,0:T(8,128)S(1)}, u32[]{:S(2)}, u32[]{:S(2)}) collective-permute-start(f32[1,32,512]{2,1,0:T(8,128)S(1)} %get-tuple-element.343), channel_id=1, source_target_pairs={{0,16},{16,32},{32,48},{48,64},{64,80},{80,96},{96,112},{1,17},{17... | collective-permute-start | bytes 196616 | tf_op jit(solution)/shard_map/ppermute | solution.py:21
  23.5 16.7 %collective-permute-start.4 = (f32[1,32,512]{2,1,0:T(8,128)S(1)}, f32[1,32,512]{2,1,0:T(8,128)}, u32[]{:S(2)}, u32[]{:S(2)}) collective-permute-start(f32[1,32,512]{2,1,0:T(8,128)S(1)} %get-tuple-element.347), channel_id=1, source_target_pairs={{0,16},{16,32},{32,48},{48,64},{64,80},{80,96},{96,112},{1,17},{17... | collective-permute-start | bytes 196616 | tf_op jit(solution)/shard_map/ppermute | solution.py:21
  24.8 7.1 %copy-start.12 = (f32[16,32,512]{2,1,0:T(8,128)S(1)}, f32[16,32,512]{2,1,0:T(8,128)}, u32[]{:S(2)}) copy-start(f32[16,32,512]{2,1,0:T(8,128)} %param.19) | copy-start | bytes 3145732
  24.8 16.4 %collective-permute-start.2 = (f32[1,32,512]{2,1,0:T(8,128)}, f32[1,32,512]{2,1,0:T(8,128)}, u32[]{:S(2)}, u32[]{:S(2)}) collective-permute-start(f32[1,32,512]{2,1,0:T(8,128)} %get-tuple-element.346), channel_id=1, source_target_pairs={{16,0},{32,16},{48,32},{64,48},{80,64},{96,80},{112,96},{17,1},{33... | collective-permute-start | bytes 196616 | tf_op jit(solution)/shard_map/ppermute | solution.py:24
  33.8 22.3 %collective-permute-start.5 = (f32[18,1,512]{2,1,0:T(1,128)}, f32[18,1,512]{2,1,0:T(1,128)S(1)}, u32[]{:S(2)}, u32[]{:S(2)}) collective-permute-start(f32[18,1,512]{2,1,0:T(1,128)} %get-tuple-element.316), channel_id=1, source_target_pairs={{1,0},{2,1},{3,2},{4,3},{5,4},{6,5},{7,6},{8,7},{9,8},{10,9},{11,1... | collective-permute-start | bytes 110600 | tf_op jit(solution)/shard_map/ppermute | solution.py:24
  38.3 17.9 %collective-permute-start.7 = (f32[18,1,512]{2,1,0:T(1,128)}, f32[18,1,512]{2,1,0:T(1,128)S(1)}, u32[]{:S(2)}, u32[]{:S(2)}) collective-permute-start(f32[18,1,512]{2,1,0:T(1,128)} %get-tuple-element.317), channel_id=1, source_target_pairs={{0,1},{1,2},{2,3},{3,4},{4,5},{5,6},{6,7},{7,8},{8,9},{9,10},{10,1... | collective-permute-start | bytes 110600 | tf_op jit(solution)/shard_map/ppermute | solution.py:21
  41.1 9.1 %copy-start.26 = (s32[3,512]{1,0:T(4,128)S(1)}, s32[3,512]{1,0:T(4,128)}, u32[]{:S(2)}) copy-start(s32[3,512]{1,0:T(4,128)} %param.20) | copy-start | bytes 18436
  42.0 8.2 %copy-start.17 = (f32[18,32,512]{2,1,0:T(8,128)}, f32[18,32,512]{2,1,0:T(8,128)S(1)}, u32[]{:S(2)}) copy-start(f32[18,32,512]{2,1,0:T(8,128)S(1)} %constant_dynamic-update-slice_fusion) | copy-start | bytes 3538948
  42.8 13.4 %collective-permute-start.6 = (f32[18,1,512]{2,1,0:T(1,128)}, f32[18,1,512]{2,1,0:T(1,128)S(1)}, u32[]{:S(2)}, u32[]{:S(2)}) collective-permute-start(f32[18,1,512]{2,1,0:T(1,128)} %get-tuple-element.318), channel_id=1, source_target_pairs={{1,0},{2,1},{3,2},{4,3},{5,4},{6,5},{7,6},{8,7},{9,8},{10,9},{11,1... | collective-permute-start | bytes 110600 | tf_op jit(solution)/shard_map/ppermute | solution.py:24
  48.3 7.9 %collective-permute-start.8 = (f32[18,1,512]{2,1,0:T(1,128)}, f32[18,1,512]{2,1,0:T(1,128)}, u32[]{:S(2)}, u32[]{:S(2)}) collective-permute-start(f32[18,1,512]{2,1,0:T(1,128)} %get-tuple-element.319), channel_id=1, source_target_pairs={{0,1},{1,2},{2,3},{3,4},{4,5},{5,6},{6,7},{7,8},{8,9},{9,10},{10,1... | collective-permute-start | bytes 110600 | tf_op jit(solution)/shard_map/ppermute | solution.py:21
  56.2 0.6 copy-start.19
  56.2 0.6 copy-start.22
  56.2 0.6 copy-start.25
  56.8 12.6 %copy-start.10 = (f32[16,32,512]{2,1,0:T(8,128)S(1)}, f32[16,32,512]{2,1,0:T(8,128)}, u32[]{:S(2)}) copy-start(f32[16,32,512]{2,1,0:T(8,128)} %add_divide_fusion.1) | copy-start | bytes 3145732
  63.5 47.4 %copy-start.4 = (f32[16,32,512]{2,1,0:T(8,128)}, f32[16,32,512]{2,1,0:T(8,128)S(1)}, u32[]{:S(2)}) copy-start(f32[16,32,512]{2,1,0:T(8,128)S(1)} %get-tuple-element.307) | copy-start | bytes 3145732
  63.5 47.4 %copy-start.6 = (f32[16,32,512]{2,1,0:T(8,128)}, f32[16,32,512]{2,1,0:T(8,128)S(1)}, u32[]{:S(2)}) copy-start(f32[16,32,512]{2,1,0:T(8,128)S(1)} %get-tuple-element.308) | copy-start | bytes 3145732
  63.6 14.2 %collective-permute-start.10 = (f32[1,32,512]{2,1,0:T(8,128)S(1)}, f32[1,32,512]{2,1,0:T(8,128)S(1)}, u32[]{:S(2)}, u32[]{:S(2)}) collective-permute-start(f32[1,32,512]{2,1,0:T(8,128)S(1)} %get-tuple-element.338), channel_id=1, source_target_pairs={{0,16},{16,32},{32,48},{48,64},{64,80},{80,96},{96,112},{1,17},{17... | collective-permute-start | bytes 196616 | tf_op jit(solution)/shard_map/ppermute | solution.py:21
  64.9 12.9 %collective-permute-start.9 = (f32[1,32,512]{2,1,0:T(8,128)S(1)}, f32[1,32,512]{2,1,0:T(8,128)S(1)}, u32[]{:S(2)}, u32[]{:S(2)}) collective-permute-start(f32[1,32,512]{2,1,0:T(8,128)S(1)} %get-tuple-element.339), channel_id=1, source_target_pairs={{16,0},{32,16},{48,32},{64,48},{80,64},{96,80},{112,96},{17,1},{33... | collective-permute-start | bytes 196616 | tf_op jit(solution)/shard_map/ppermute | solution.py:24
  70.1 82.8 %collective-permute-start.24 = (f32[16,1,512]{2,1,0:T(1,128)}, f32[16,1,512]{2,1,0:T(1,128)}, u32[]{:S(2)}, u32[]{:S(2)}) collective-permute-start(f32[16,1,512]{2,1,0:T(1,128)} %get-tuple-element.324), channel_id=1, source_target_pairs={{1,0},{2,1},{3,2},{4,3},{5,4},{6,5},{7,6},{8,7},{9,8},{10,9},{11,1... | collective-permute-start | bytes 98312 | tf_op jit(solution)/shard_map/ppermute | solution.py:24
  75.8 77.1 %collective-permute-start.25 = (f32[16,1,512]{2,1,0:T(1,128)}, f32[16,1,512]{2,1,0:T(1,128)}, u32[]{:S(2)}, u32[]{:S(2)}) collective-permute-start(f32[16,1,512]{2,1,0:T(1,128)} %get-tuple-element.325), channel_id=1, source_target_pairs={{0,1},{1,2},{2,3},{3,4},{4,5},{5,6},{6,7},{7,8},{8,9},{9,10},{10,1... | collective-permute-start | bytes 98312 | tf_op jit(solution)/shard_map/ppermute | solution.py:21
  77.8 8.0 %collective-permute-start.11 = (f32[18,1,512]{2,1,0:T(1,128)S(1)}, f32[18,1,512]{2,1,0:T(1,128)S(1)}, u32[]{:S(2)}, u32[]{:S(2)}) collective-permute-start(f32[18,1,512]{2,1,0:T(1,128)S(1)} %get-tuple-element.314), channel_id=1, source_target_pairs={{1,0},{2,1},{3,2},{4,3},{5,4},{6,5},{7,6},{8,7},{9,8},{10,9},{11,1... | collective-permute-start | bytes 110600 | tf_op jit(solution)/shard_map/ppermute | solution.py:24
  83.3 7.0 %copy-start.8 = (f32[16,32,512]{2,1,0:T(8,128)S(1)}, f32[16,32,512]{2,1,0:T(8,128)}, u32[]{:S(2)}) copy-start(f32[16,32,512]{2,1,0:T(8,128)} %get-tuple-element.297) | copy-start | bytes 3145732
  83.3 7.0 %copy-start.20 = (f32[18,1,512]{2,1,0:T(1,128)S(1)}, f32[18,1,512]{2,1,0:T(1,128)}, u32[]{:S(2)}) copy-start(f32[18,1,512]{2,1,0:T(1,128)} %copy-done.19) | copy-start | bytes 110596
  83.3 7.0 %copy-start.23 = (f32[18,1,512]{2,1,0:T(1,128)S(1)}, f32[18,1,512]{2,1,0:T(1,128)}, u32[]{:S(2)}) copy-start(f32[18,1,512]{2,1,0:T(1,128)} %copy-done.22) | copy-start | bytes 110596
  83.4 6.9 %collective-permute-start.12 = (f32[18,1,512]{2,1,0:T(1,128)S(1)}, f32[18,1,512]{2,1,0:T(1,128)S(1)}, u32[]{:S(2)}, u32[]{:S(2)}) collective-permute-start(f32[18,1,512]{2,1,0:T(1,128)S(1)} %get-tuple-element.315), channel_id=1, source_target_pairs={{0,1},{1,2},{2,3},{3,4},{4,5},{5,6},{6,7},{7,8},{8,9},{9,10},{10,1... | collective-permute-start | bytes 110600 | tf_op jit(solution)/shard_map/ppermute | solution.py:21
  93.3 8.6 %collective-permute-start.13 = (f32[1,32,512]{2,1,0:T(8,128)S(1)}, f32[1,32,512]{2,1,0:T(8,128)S(1)}, u32[]{:S(2)}, u32[]{:S(2)}) collective-permute-start(f32[1,32,512]{2,1,0:T(8,128)S(1)} %get-tuple-element.335), channel_id=1, source_target_pairs={{16,0},{32,16},{48,32},{64,48},{80,64},{96,80},{112,96},{17,1},{33... | collective-permute-start | bytes 196616 | tf_op jit(solution)/shard_map/ppermute | solution.py:24
  99.0 3.1 collective-permute-start.14
  102.2 5.9 %collective-permute-start.15 = (f32[18,1,512]{2,1,0:T(1,128)S(1)}, f32[18,1,512]{2,1,0:T(1,128)S(1)}, u32[]{:S(2)}, u32[]{:S(2)}) collective-permute-start(f32[18,1,512]{2,1,0:T(1,128)S(1)} %get-tuple-element.312), channel_id=1, source_target_pairs={{1,0},{2,1},{3,2},{4,3},{5,4},{6,5},{7,6},{8,7},{9,8},{10,9},{11,1... | collective-permute-start | bytes 110600 | tf_op jit(solution)/shard_map/ppermute | solution.py:24
  104.1 6.8 %collective-permute-start.16 = (f32[18,1,512]{2,1,0:T(1,128)S(1)}, f32[18,1,512]{2,1,0:T(1,128)S(1)}, u32[]{:S(2)}, u32[]{:S(2)}) collective-permute-start(f32[18,1,512]{2,1,0:T(1,128)S(1)} %get-tuple-element.313), channel_id=1, source_target_pairs={{0,1},{1,2},{2,3},{3,4},{4,5},{5,6},{6,7},{7,8},{8,9},{9,10},{10,1... | collective-permute-start | bytes 110600 | tf_op jit(solution)/shard_map/ppermute | solution.py:21
  110.9 13.6 %copy-start.13 = (f32[16,32,512]{2,1,0:T(8,128)S(1)}, f32[16,32,512]{2,1,0:T(8,128)}, u32[]{:S(2)}) copy-start(f32[16,32,512]{2,1,0:T(8,128)} %param.19) | copy-start | bytes 3145732
  113.9 1.1 copy-start.2
  115.6 9.9 %collective-permute-start.17 = (f32[1,32,512]{2,1,0:T(8,128)}, f32[1,32,512]{2,1,0:T(8,128)}, u32[]{:S(2)}, u32[]{:S(2)}) collective-permute-start(f32[1,32,512]{2,1,0:T(8,128)} %get-tuple-element.331), channel_id=1, source_target_pairs={{16,0},{32,16},{48,32},{64,48},{80,64},{96,80},{112,96},{17,1},{33... | collective-permute-start | bytes 196616 | tf_op jit(solution)/shard_map/ppermute | solution.py:24
  121.8 3.7 collective-permute-start.18
  125.5 6.8 %copy-start.3 = (f32[16,32,512]{2,1,0:T(8,128)S(1)}, f32[16,32,512]{2,1,0:T(8,128)}, u32[]{:S(2)}) copy-start(f32[16,32,512]{2,1,0:T(8,128)} %copy-done.2) | copy-start | bytes 3145732
  126.7 6.0 %collective-permute-start.19 = (f32[18,1,512]{2,1,0:T(1,128)S(1)}, f32[18,1,512]{2,1,0:T(1,128)S(1)}, u32[]{:S(2)}, u32[]{:S(2)}) collective-permute-start(f32[18,1,512]{2,1,0:T(1,128)S(1)} %get-tuple-element.310), channel_id=1, source_target_pairs={{1,0},{2,1},{3,2},{4,3},{5,4},{6,5},{7,6},{8,7},{9,8},{10,9},{11,1... | collective-permute-start | bytes 110600 | tf_op jit(solution)/shard_map/ppermute | solution.py:24
  128.7 7.1 %copy-start.5 = (f32[16,32,512]{2,1,0:T(8,128)S(1)}, f32[16,32,512]{2,1,0:T(8,128)}, u32[]{:S(2)}) copy-start(f32[16,32,512]{2,1,0:T(8,128)} %copy-done.4) | copy-start | bytes 3145732
  128.7 7.1 %copy-start.7 = (f32[16,32,512]{2,1,0:T(8,128)S(1)}, f32[16,32,512]{2,1,0:T(8,128)}, u32[]{:S(2)}) copy-start(f32[16,32,512]{2,1,0:T(8,128)} %copy-done.6) | copy-start | bytes 3145732
  128.7 7.1 %copy-start.9 = (f32[16,32,512]{2,1,0:T(8,128)S(1)}, f32[16,32,512]{2,1,0:T(8,128)}, u32[]{:S(2)}) copy-start(f32[16,32,512]{2,1,0:T(8,128)} %get-tuple-element.297) | copy-start | bytes 3145732
  128.7 7.1 %copy-start.21 = (f32[18,1,512]{2,1,0:T(1,128)S(1)}, f32[18,1,512]{2,1,0:T(1,128)}, u32[]{:S(2)}) copy-start(f32[18,1,512]{2,1,0:T(1,128)} %copy-done.19) | copy-start | bytes 110596
  128.7 7.1 %copy-start.24 = (f32[18,1,512]{2,1,0:T(1,128)S(1)}, f32[18,1,512]{2,1,0:T(1,128)}, u32[]{:S(2)}) copy-start(f32[18,1,512]{2,1,0:T(1,128)} %copy-done.22) | copy-start | bytes 110596
  128.7 7.1 %collective-permute-start.20 = (f32[18,1,512]{2,1,0:T(1,128)S(1)}, f32[18,1,512]{2,1,0:T(1,128)S(1)}, u32[]{:S(2)}, u32[]{:S(2)}) collective-permute-start(f32[18,1,512]{2,1,0:T(1,128)S(1)} %get-tuple-element.311), channel_id=1, source_target_pairs={{0,1},{1,2},{2,3},{3,4},{4,5},{5,6},{6,7},{7,8},{8,9},{9,10},{10,1... | collective-permute-start | bytes 110600 | tf_op jit(solution)/shard_map/ppermute | solution.py:21
  139.6 18.5 %copy-start.1 = (f32[16,32,512]{2,1,0:T(8,128)}, f32[16,32,512]{2,1,0:T(8,128)S(1)}, u32[]{:S(2)}) copy-start(f32[16,32,512]{2,1,0:T(8,128)S(1)} %fusion.63) | copy-start | bytes 3145732
  139.7 13.2 %collective-permute-start.21 = (f32[16,1,512]{2,1,0:T(1,128)S(1)}, f32[16,1,512]{2,1,0:T(1,128)S(1)}, u32[]{:S(2)}, u32[]{:S(2)}) collective-permute-start(f32[16,1,512]{2,1,0:T(1,128)S(1)} %get-tuple-element.326), channel_id=1, source_target_pairs={{0,1},{1,2},{2,3},{3,4},{4,5},{5,6},{6,7},{7,8},{8,9},{9,10},{10,1... | collective-permute-start | bytes 98312 | tf_op jit(solution)/shard_map/ppermute | solution.py:21
  141.6 11.3 %copy-start.11 = (f32[16,32,512]{2,1,0:T(8,128)S(1)}, f32[16,32,512]{2,1,0:T(8,128)}, u32[]{:S(2)}) copy-start(f32[16,32,512]{2,1,0:T(8,128)} %add_divide_fusion.1) | copy-start | bytes 3145732
  141.6 11.3 %copy-start.14 = (f32[16,32,511]{2,1,0:T(8,128)S(1)}, f32[16,32,511]{2,1,0:T(8,128)}, u32[]{:S(2)}) copy-start(f32[16,32,511]{2,1,0:T(8,128)} %get-tuple-element.322) | copy-start | bytes 3139588
  141.6 11.3 %copy-start.15 = (f32[16,32,511]{2,1,0:T(8,128)S(1)}, f32[16,32,511]{2,1,0:T(8,128)}, u32[]{:S(2)}) copy-start(f32[16,32,511]{2,1,0:T(8,128)} %get-tuple-element.323) | copy-start | bytes 3139588
  141.7 11.3 %collective-permute-start.22 = (f32[16,1,512]{2,1,0:T(1,128)S(1)}, f32[16,1,512]{2,1,0:T(1,128)S(1)}, u32[]{:S(2)}, u32[]{:S(2)}) collective-permute-start(f32[16,1,512]{2,1,0:T(1,128)S(1)} %get-tuple-element.327), channel_id=1, source_target_pairs={{1,0},{2,1},{3,2},{4,3},{5,4},{6,5},{7,6},{8,7},{9,8},{10,9},{11,1... | collective-permute-start | bytes 98312 | tf_op jit(solution)/shard_map/ppermute | solution.py:24
  147.8 10.3 %collective-permute-start.23 = (f32[1,32,512]{2,1,0:T(8,128)S(1)}, f32[1,32,512]{2,1,0:T(8,128)S(1)}, u32[]{:S(2)}, u32[]{:S(2)}) collective-permute-start(f32[1,32,512]{2,1,0:T(8,128)S(1)} %slice.403), channel_id=1, source_target_pairs={{16,0},{32,16},{48,32},{64,48},{80,64},{96,80},{112,96},{17,1},{33... | collective-permute-start | bytes 196616 | tf_op jit(solution)/shard_map/ppermute | solution.py:32
  152.9 5.2 %copy-start.18 = (f32[16,32,512]{2,1,0:T(8,128)S(1)}, f32[16,32,512]{2,1,0:T(8,128)}, u32[]{:S(2)}) copy-start(f32[16,32,512]{2,1,0:T(8,128)} %param.17) | copy-start | bytes 3145732
  158.1 1.1 copy-start.16
  159.2 3.3 collective-permute-start
  162.6 5.3 %collective-permute-start = (f32[32,512]{1,0:T(8,128)}, f32[32,512]{1,0:T(8,128)S(1)}, u32[]{:S(2)}, u32[]{:S(2)}) collective-permute-start(f32[32,512]{1,0:T(8,128)} %get-tuple-element.539), channel_id=1, source_target_pairs={{0,16},{16,32},{32,48},{48,64},{64,80},{80,96},{96,112},{1,17},{17... | collective-permute-start | bytes 196616 | tf_op jit(solution)/shard_map/while/body/eval_jaxpr/ppermute | solution.py:32
  167.9 5.8 %collective-permute-start = (f32[32,512]{1,0:T(8,128)}, f32[32,512]{1,0:T(8,128)S(1)}, u32[]{:S(2)}, u32[]{:S(2)}) collective-permute-start(f32[32,512]{1,0:T(8,128)} %get-tuple-element.539), channel_id=1, source_target_pairs={{0,16},{16,32},{32,48},{48,64},{64,80},{80,96},{96,112},{1,17},{17... | collective-permute-start | bytes 196616 | tf_op jit(solution)/shard_map/while/body/eval_jaxpr/ppermute | solution.py:32
  173.6 5.8 %collective-permute-start = (f32[32,512]{1,0:T(8,128)}, f32[32,512]{1,0:T(8,128)S(1)}, u32[]{:S(2)}, u32[]{:S(2)}) collective-permute-start(f32[32,512]{1,0:T(8,128)} %get-tuple-element.539), channel_id=1, source_target_pairs={{0,16},{16,32},{32,48},{48,64},{64,80},{80,96},{96,112},{1,17},{17... | collective-permute-start | bytes 196616 | tf_op jit(solution)/shard_map/while/body/eval_jaxpr/ppermute | solution.py:32
  179.4 5.8 %collective-permute-start = (f32[32,512]{1,0:T(8,128)}, f32[32,512]{1,0:T(8,128)S(1)}, u32[]{:S(2)}, u32[]{:S(2)}) collective-permute-start(f32[32,512]{1,0:T(8,128)} %get-tuple-element.539), channel_id=1, source_target_pairs={{0,16},{16,32},{32,48},{48,64},{64,80},{80,96},{96,112},{1,17},{17... | collective-permute-start | bytes 196616 | tf_op jit(solution)/shard_map/while/body/eval_jaxpr/ppermute | solution.py:32
  185.2 5.8 %collective-permute-start = (f32[32,512]{1,0:T(8,128)}, f32[32,512]{1,0:T(8,128)S(1)}, u32[]{:S(2)}, u32[]{:S(2)}) collective-permute-start(f32[32,512]{1,0:T(8,128)} %get-tuple-element.539), channel_id=1, source_target_pairs={{0,16},{16,32},{32,48},{48,64},{64,80},{80,96},{96,112},{1,17},{17... | collective-permute-start | bytes 196616 | tf_op jit(solution)/shard_map/while/body/eval_jaxpr/ppermute | solution.py:32
  191.0 262.3 %collective-permute-start = (f32[32,512]{1,0:T(8,128)}, f32[32,512]{1,0:T(8,128)S(1)}, u32[]{:S(2)}, u32[]{:S(2)}) collective-permute-start(f32[32,512]{1,0:T(8,128)} %get-tuple-element.539), channel_id=1, source_target_pairs={{0,16},{16,32},{32,48},{48,64},{64,80},{80,96},{96,112},{1,17},{17... | collective-permute-start | bytes 196616 | tf_op jit(solution)/shard_map/while/body/eval_jaxpr/ppermute | solution.py:32
  492.1 3.3 collective-permute-start
where the time goes:
time: 499 us; the launch traced here: 495 us
  waiting for transfers between devices  298 us (60%)
  starting transfers between devices  92.6 us (19%)
  other arithmetic  83.7 us (17%)
  local copies, waits for them, and re-layouts  20 us (4%)
    ppermute x9, waiting for transfers between devices, passed_along(): return lax.ppermute(value, axis, pairs)  287 us
    ppermute x12, starting transfers between devices, padded(): lax.ppermute(lax.slice_in_dim(block, 0, width, axis=dim), axis, backward)  54 us
    dynamic_update_slice x16, other arithmetic, sweep(): lax.scan(advance, inflow, (volume, through, explicit, old_sat))  27.8 us
    ppermute x12, starting transfers between devices, padded(): lax.ppermute(lax.slice_in_dim(block, block.shape[dim] - width, None, axis...  23.3 us
    add x4, other arithmetic, jacobi(): return center + OMEGA * (source - storage * center - flow) / diagonal  16.5 us
    ppermute x9, starting transfers between devices, passed_along(): return lax.ppermute(value, axis, pairs)  15.3 us
    ppermute x12, waiting for transfers between devices, padded(): lax.ppermute(lax.slice_in_dim(block, block.shape[dim] - width, None, axis...  10.6 us
    mul x16, other arithmetic, advance(): return (flux_row * fraction(water), water)  10.4 us
  transfers between devices with their start and end apart: 33, of which 12 were waited for; matrix products, arithmetic and copies ran while one was open for 7% of the time, Pallas kernels for 0%

commit v1 on v0

v1 whole, which is shorter than its diff:
```python
import functools

import jax
import jax.numpy as jnp
from jax import lax
from jax.experimental import pallas as pl
from jax.experimental.pallas import tpu as pltpu
from jax.sharding import PartitionSpec as P

PASSES = 4
MOBILITY = 0.5
OMEGA = 0.8
VOLUME = 4.0
COMPRESS = 0.5

MESH = pl.DeviceIdType.MESH
LX = 16
NL = 32
EL = 41
LO = 4
ER = 40
RO = 12
ROCKS = 8
FAR = 1e30
NXC = 4
NGY = 16
WELLS = 512


def roll(value, shift):
    return pltpu.roll(value, shift % 128, 1)


def next_z(tiles):
    return [tiles[1], tiles[2], tiles[3], roll(tiles[0], -1)]


def prev_z(tiles):
    return [roll(tiles[3], 1), tiles[0], tiles[1], tiles[2]]


def layers(start, stop, block, body):
    whole = (stop - start) // block

    def several(i, _):
        for j in range(block):
            body(start + block * i + j)
        return 0

    lax.fori_loop(0, whole, several, 0)
    for l in range(start + block * whole, stop):
        body(l)


def recip(value):
    return pl.reciprocal(value, approx=False)


def permuted(value, matrix, parts):
    total, rest = None, value
    for k in range(parts):
        piece = rest.astype(jnp.bfloat16)
        term = jnp.dot(piece, matrix, preferred_element_type=jnp.float32)
        total = term if total is None else total + term
        if k < parts - 1:
            rest = rest - piece.astype(jnp.float32)
    return total


def lanes(z):
    return slice(128 * z, 128 * z + 128)


def step_kernel(
    rock, perm_tab, poro_tab, base, press, sat0, wells, well_rates,
    out_p, out_s,
    st_r, st_p, st_s, st_b,
    in_r, in_p, in_s, in_b, my_r, my_p, my_s, my_b, pk_r, pk_p, pk_s, pk_c, ys_r, ys_p, ys_s, co,
    hh, st, pa, pb, te, tn, tb, ww, src, rt, hot_a, hot_b, fs, order, back,
    face_in, face_out, res_p, res_s,
    loc, snd, rcv,
):
    gx, gy = lax.axis_index("gx"), lax.axis_index("gy")
    xc, core = gx // 2, lax.rem(gx, 2)
    partner = (gx + 1 - 2 * core, gy)
    low, high = xc > 0, xc < NXC - 1
    down, up = gy > 0, gy < NGY - 1
    f32 = jnp.float32

    barrier = pltpu.get_barrier_semaphore()
    count = jnp.int32(0)
    for dx in (-1, 0, 1):
        for dy in (-1, 0, 1):
            for other in (0, 1):
                there = (xc + dx >= 0) & (xc + dx < NXC) & (gy + dy >= 0) & (gy + dy < NGY)
                if dx == 0 and dy == 0:
                    there = there & (core != other)
                count = count + there.astype(jnp.int32)

                @pl.when(there)
                def _(dx=dx, dy=dy, other=other):
                    pl.semaphore_signal(
                        barrier, inc=1, device_id=(2 * (xc + dx) + other, gy + dy), device_id_type=MESH
                    )

    def local(k, a, b):
        return pltpu.make_async_copy(a, b, loc.at[k])

    row24 = pl.ds(pl.multiple_of(8 * core, 8), 24)
    row16 = pl.ds(pl.multiple_of(16 * core, 16), 16)
    own = pl.ds(LO + LX * core, LX)
    own0 = pl.ds(LX * core, LX)
    loads = [
        local(0, rock, in_r), local(1, press, in_p), local(2, sat0, in_s), local(3, base, in_b)
    ]
    for copy in loads:
        copy.start()
    blocks = [
        local(4, my_r.at[:, row24, :], st_r.at[own]),
        local(5, my_p.at[:, row24, :], st_p.at[own]),
        local(6, my_s.at[:, row24, :], st_s.at[own0]),
        local(7, my_b.at[:, row16, :], st_b.at[own0]),
    ]

    def remote(k, j, a, b, device):
        return pltpu.make_async_remote_copy(
            src_ref=a, dst_ref=b, send_sem=snd.at[k], recv_sem=rcv.at[j], device_id=device, device_id_type=MESH
        )

    other24 = pl.ds(pl.multiple_of(8 * (1 - core), 8), 24)
    other16 = pl.ds(pl.multiple_of(16 * (1 - core), 16), 16)
    sends = []
    ypart = pl.ds(pl.multiple_of(LX * core, 16), LX)
    last_layers, first_layers = (core == 1) & high, (core == 0) & low
    for k, (a, b, pk, ys) in enumerate(((my_r, st_r, pk_r, ys_r), (my_p, st_p, pk_p, ys_p))):
        for side, ok, device in ((0, down, (2 * xc + 1, gy - 1)), (1, up, (2 * xc, gy + 1))):
            sends.append((ok, remote(4 + 2 * k + side, 4 + k, pk.at[side], ys.at[:, ypart, :], device)))
        for d in (0, 1):
            rows, place = pl.ds(16 * d, 16), pl.ds(8 * d, 16)
            sends.append((last_layers, remote(
                8 + 2 * d + k, 7 + k, a.at[pl.ds(12, 4), rows, :], b.at[pl.ds(0, 4), place, :], (2 * (xc + 1) + d, gy),
            )))
            sends.append((first_layers, remote(
                8 + 2 * d + k, 9 + k, a.at[pl.ds(0, 5), rows, :], b.at[pl.ds(LO + NL, 5), place, :], (2 * (xc - 1) + d, gy),
            )))
        sends.append((None, remote(k, k, a.at[:, other24, :], b.at[own], partner)))
    for group, (ok, d, dy, kind) in enumerate(((down, 1, -1, 0), (up, 0, 1, 0), (None, 1, 0, 1), (None, 0, 0, 1))):
        for part, side, dx in ((last_layers, 0, 1), (first_layers, 1, -1)):
            sends.append((
                part if ok is None else part & ok,
                remote(12 + group, 11 + 2 * kind + side, pk_c.at[group], co.at[kind, side], (2 * (xc + dx) + d, gy + dy)),
            ))
    sends_late = []
    for side, ok, device in ((0, down, (2 * xc + 1, gy - 1)), (1, up, (2 * xc, gy + 1))):
        sends_late.append((ok, remote(16 + side, 6, pk_s.at[side], ys_s.at[ypart, :], device)))
    sends_late.append((None, remote(2, 2, my_s.at[:, other24, :], st_s.at[own0], partner)))
    sends_late.append((None, remote(3, 3, my_b.at[:, other16, :], st_b.at[own0], partner)))

    def guarded(ok, action):
        if ok is None:
            action()
        else:
            pl.when(ok)(action)

    def arrived(k, ref, ok=None):
        guarded(ok, lambda: pltpu.make_async_copy(ref, ref, rcv.at[k]).wait())

    outer = ((core == 0) & down) | ((core == 1) & up)

    def depth_of(place):
        return 4 * lax.rem(place, 128) + place // 128

    ahead = lax.broadcasted_iota(jnp.int32, (512, 512), 0)
    aside = lax.broadcasted_iota(jnp.int32, (512, 512), 1)
    order[...] = jnp.where(ahead == depth_of(aside), 1.0, 0.0).astype(jnp.bfloat16)
    back[...] = jnp.where(depth_of(ahead) == aside, 1.0, 0.0).astype(jnp.bfloat16)

    def reorder(a, b, parts):
        def body(m, _):
            at = pl.ds(pl.multiple_of(8 * m, 8), 8)
            value = a[at].reshape(256, 512).astype(f32)
            b[at] = permuted(value, order[...], parts).reshape(8, 32, 512)
            return 0

        lax.fori_loop(0, 2, body, 0)

    loads[0].wait()
    reorder(in_r, my_r, 1)
    loads[1].wait()
    reorder(in_p, my_p, 3)
    for side in (0, 1):
        for a, b in ((my_r, pk_r), (my_p, pk_p)):
            for r in range(5):
                b[side, r] = a[:, r + 27 * side, :]

    def by_core(action):
        for c in (0, 1):
            pl.when(core == c)(functools.partial(action, c))

    def pack_corners(c):
        part = slice(12, 16) if c == 1 else slice(0, 4)
        for group, row in enumerate((0, 28, 12, 16)):
            for k, a in enumerate((my_r, my_p)):
                for r in range(4):
                    for z in range(4):
                        pk_c[group, k, r, 4 * z : 4 * z + 4, :] = a[part, row + r, lanes(z)]

    by_core(pack_corners)
    blocks[0].start()
    blocks[1].start()
    pl.semaphore_wait(barrier, count)
    for ok, copy in sends:
        guarded(ok, copy.start)
    loads[2].wait()
    reorder(in_s, my_s, 3)
    for side in (0, 1):
        pk_s[side] = my_s[:, 31 * side, :]
    loads[3].wait()
    reorder(in_b, my_b, 3)
    blocks[2].start()
    blocks[3].start()
    for ok, copy in sends_late:
        guarded(ok, copy.start)

    @pl.when(jnp.logical_not(low))
    def _():
        st_r[0:LO] = jnp.full((LO, 24, 512), float(ROCKS), f32)
        st_p[0:LO] = jnp.zeros((LO, 24, 512), f32)

    @pl.when(jnp.logical_not(high))
    def _():
        st_r[LO + NL :] = jnp.full((5, 24, 512), float(ROCKS), f32)
        st_p[LO + NL :] = jnp.zeros((5, 24, 512), f32)

    @pl.when(jnp.logical_not(outer))
    def _():
        ys_r[...] = jnp.full((5, NL, 512), float(ROCKS), f32)
        ys_p[...] = jnp.zeros((5, NL, 512), f32)
        ys_s[...] = jnp.zeros((NL, 512), f32)

    for side, ok in ((0, low), (1, high)):

        @pl.when(jnp.logical_not(ok & outer))
        def _(side=side):
            co[0, side, 0] = jnp.full((4, 16, 128), float(ROCKS), f32)
            co[0, side, 1] = jnp.zeros((4, 16, 128), f32)

        @pl.when(jnp.logical_not(ok))
        def _(side=side):
            co[1, side, 0] = jnp.full((4, 16, 128), float(ROCKS), f32)
            co[1, side, 1] = jnp.zeros((4, 16, 128), f32)

    well_x, well_y, well_z = wells[0:1, :], wells[1:2, :], wells[2:3, :]
    rate = well_rates[...]
    x0, y0 = NL * xc - LO, NL * gy + LX * core - 4
    columns = depth_of(lax.broadcasted_iota(jnp.int32, (512, WELLS), 0))
    one_z = jnp.where(columns == well_z, 1.0, 0.0).astype(jnp.bfloat16)
    hot_b[:, 0:WELLS] = one_z
    hot_b[:, WELLS:] = one_z
    pair_ids = lax.broadcasted_iota(jnp.int32, (48, WELLS), 0)
    second = pair_ids >= 24
    row_ids = jnp.where(second, pair_ids - 24, pair_ids) + y0
    layer_ids = jnp.where(second, 1, 0) + x0
    high_part = rate.astype(jnp.bfloat16).astype(f32)
    low_part = rate - high_part

    def hot_rows(l, _):
        here = (row_ids == well_y) & (layer_ids == well_x - 2 * l)
        at = pl.ds(pl.multiple_of(48 * l, 16), 48)
        hot_a[at, 0:WELLS] = jnp.where(here, high_part, 0.0).astype(jnp.bfloat16)
        hot_a[at, WELLS:] = jnp.where(here, low_part, 0.0).astype(jnp.bfloat16)
        return 0

    lax.fori_loop(0, (EL + 1) // 2, hot_rows, 0)

    def spread(m, _):
        at = pl.ds(pl.multiple_of(336 * m, 16), 336)
        got = lax.dot_general(
            hot_a[at, :], hot_b[...], (((1,), (1,)), ((), ())), preferred_element_type=f32
        )
        for z in range(4):
            rt[z, pl.ds(14 * m, 14)] = got[:, lanes(z)].reshape(14, 24, 128)
        return 0

    lax.fori_loop(0, 3, spread, 0)

    def table(ref, rule):
        return [rule(jnp.full((8, 128), ref[k], f32)) for k in range(ROCKS)]

    tab_h = table(perm_tab, lambda v: 0.5 / v) + [jnp.full((8, 128), FAR, f32)]
    tab_s = table(poro_tab, lambda v: (COMPRESS * VOLUME) * v) + [jnp.full((8, 128), 1.0, f32)]

    def lookup(kinds, n=8):
        h, s = tab_h[0][:n], tab_s[0][:n]
        for k in range(1, ROCKS + 1):
            later = kinds > k - 0.5
            h = jnp.where(later, tab_h[k][:n], h)
            s = jnp.where(later, tab_s[k][:n], s)
        return h, s

    def unpack_layers(first, last, at_row, tiles=(0, 1, 2)):
        def body(l, _):
            for z in range(4):
                for t in tiles:
                    h, s = lookup(st_r[l, 8 * t : 8 * t + 8, lanes(z)])
                    e = at_row + 8 * t
                    hh[z, l, e : e + 8, :] = h
                    st[z, l, e : e + 8, :] = s
                    pa[z, l, e : e + 8, :] = st_p[l, 8 * t : 8 * t + 8, lanes(z)]
            return 0

        lax.fori_loop(first, last, body, 0)

    for copy in blocks:
        copy.wait()
    arrived(0, st_r.at[pl.ds(LO, LX)])
    arrived(1, st_p.at[pl.ds(LO, LX)])
    by_core(lambda c: unpack_layers(LO, LO + NL, RO - 8 * c))

    def fraction(s):
        q = s * s
        return q * recip(1.5 * q + (0.5 - s))

    arrived(2, st_s.at[pl.ds(0, LX)])
    arrived(3, st_b.at[pl.ds(0, LX)])

    def unpack_fraction(c):
        def body(l, _):
            for z in range(4):
                for t in range(3):
                    e = 8 - 8 * c + 8 * t
                    fs[z, l, e : e + 8, :] = fraction(st_s[l, 8 * t : 8 * t + 8, lanes(z)])
            return 0

        lax.fori_loop(0, NL, body, 0)

    by_core(unpack_fraction)

    arrived(4, ys_r, outer)
    arrived(5, ys_p, outer)
    arrived(6, ys_s, outer)
    rows_here = pl.ds(pl.multiple_of(8 * core, 8), 16)
    arrived(7, st_r.at[pl.ds(0, 4), rows_here, :], low)
    arrived(8, st_p.at[pl.ds(0, 4), rows_here, :], low)
    arrived(9, st_r.at[pl.ds(LO + NL, 5), rows_here, :], high)
    arrived(10, st_p.at[pl.ds(LO + NL, 5), rows_here, :], high)
    arrived(11, co.at[0, 0], low & outer)
    arrived(12, co.at[0, 1], high & outer)
    arrived(13, co.at[1, 0], low)
    arrived(14, co.at[1, 1], high)

    def unpack_halo(c):
        unpack_layers(0, LO, RO - 8 * c, (c, c + 1))
        unpack_layers(LO + NL, EL, RO - 8 * c, (c, c + 1))
        e = 7 if c == 0 else 28

        for z in range(4):
            for r in range(5):
                for g in range(4):
                    at = pl.ds(LO + 8 * g, 8)
                    h, s = lookup(ys_r[r, 8 * g : 8 * g + 8, lanes(z)])
                    hh[z, at, e + r, :] = h
                    st[z, at, e + r, :] = s
                    pa[z, at, e + r, :] = ys_p[r, 8 * g : 8 * g + 8, lanes(z)]
            for kind in (0, 1):
                e4 = 8 if c == kind else 28
                for r in range(4):
                    for side, place in ((0, 0), (1, LO + NL)):
                        at = pl.ds(place, 4)
                        h, s = lookup(co[kind, side, 0, r, 4 * z : 4 * z + 4, :], 4)
                        hh[z, at, e4 + r, :] = h
                        st[z, at, e4 + r, :] = s
                        pa[z, at, e4 + r, :] = co[kind, side, 1, r, 4 * z : 4 * z + 4, :]
            fs[z, :, 7 if c == 0 else 24, :] = fraction(ys_s[:, lanes(z)])

    by_core(unpack_halo)

    lane = lax.broadcasted_iota(jnp.int32, (24, 128), 1)
    last = lane == 127

    def side_faces(l):
        for z in range(4):
            te[z, l, 8:32, :] = recip(hh[z, l, 8:32, :] + hh[z, l + 1, 8:32, :])
            tn[z, l, 0:32, :] = recip(hh[z, l, 0:32, :] + hh[z, l, 1:33, :])

    layers(0, EL - 1, 2, side_faces)

    def weights(l):
        own_h = [hh[z, l, 8:32, :] for z in range(4)]
        deeper = next_z(own_h)
        below = [recip(own_h[z] + deeper[z]) for z in range(4)]
        below[3] = jnp.where(last, 0.0, below[3])
        above = prev_z(below)
        for z in (1, 2, 3, 0):
            tb[z, l, 8:32, :] = below[z]
            storage = st[z, l, 8:32, :]
            diagonal = (
                storage + te[z, l, 8:32, :] + te[z, l - 1, 8:32, :]
                + tn[z, l, 8:32, :] + tn[z, l, 7:31, :] + below[z] + above[z]
            )
            ww[z, l, 8:32, :] = OMEGA * recip(diagonal)
            src[z, l, 8:32, :] = storage * pa[z, l, 8:32, :] + rt[z, l]

    layers(1, EL - 1, 3, weights)

    def one_pass(old, new, start, stop):
        def body(l):
            here = [old[z, l, 8:32, :] for z in range(4)]
            faces = [tb[z, l, 8:32, :] for z in range(4)]
            deeper = next_z(here)
            shallower = prev_z([faces[z] * here[z] for z in range(4)])
            for z in (1, 2, 3, 0):
                total = (
                    src[z, l, 8:32, :] + faces[z] * deeper[z] + shallower[z]
                    + te[z, l, 8:32, :] * old[z, l + 1, 8:32, :]
                    + te[z, l - 1, 8:32, :] * old[z, l - 1, 8:32, :]
                    + tn[z, l, 8:32, :] * old[z, l, 9:33, :]
                    + tn[z, l, 7:31, :] * old[z, l, 7:31, :]
                )
                new[z, l, 8:32, :] = (1.0 - OMEGA) * here[z] + ww[z, l, 8:32, :] * total

        layers(start, stop, 3, body)

    one_pass(pa, pb, 1, 40)
    one_pass(pb, pa, 2, 39)
    one_pass(pa, pb, 3, 38)
    one_pass(pb, pa, 4, 37)

    def fluxes(l):
        e = l + LO
        center = [pa[z, e, RO : RO + 16, :] for z in range(4)]
        frac = [fs[z, l, 8:24, :] for z in range(4)]
        deeper, frac_deep = next_z(center), next_z(frac)
        drained = []
        for z in range(4):
            flow = tb[z, e, RO : RO + 16, :] * (center[z] - deeper[z])
            drained.append(flow * jnp.where(flow > 0, frac[z], frac_deep[z]))
        entered = prev_z(drained)
        at = pl.ds(pl.multiple_of(8 * core, 8), 16)
        for z in range(4):
            p, f = center[z], frac[z]
            res_p[l, :, lanes(z)] = p
            through = jnp.maximum(
                st_b[l, :, lanes(z)] + te[z, e, RO : RO + 16, :] * (p - pa[z, e + 1, RO : RO + 16, :]), 0.0
            )
            north = tn[z, e, RO : RO + 16, :] * (p - pa[z, e, RO + 1 : RO + 17, :])
            south = tn[z, e, RO - 1 : RO + 15, :] * (p - pa[z, e, RO - 1 : RO + 15, :])
            leaving = drained[z] - entered[z]
            leaving = leaving + north * jnp.where(north > 0, f, fs[z, l, 9:25, :])
            leaving = leaving + south * jnp.where(south > 0, f, fs[z, l, 7:23, :])
            rates = rt[z, e, 4:20, :]
            extra = rates * jnp.where(rates > 0, 1.0, f) - leaving
            per_volume = recip((1.0 / COMPRESS) * st[z, e, RO : RO + 16, :])
            s = st_s[l, at, lanes(z)]
            q = s * s
            inverse = recip(1.5 * q + (0.5 - s))
            slope = (s - q) * inverse * inverse
            extra = extra * per_volume
            relative = through * per_volume
            step = recip(1.0 + relative * slope)
            hh[z, l, 8:24, :] = s + extra
            hh[z, l, 24:40, :] = per_volume
            pb[z, l, 8:24, :] = s + (extra - relative * f) * step
            pb[z, l, 24:40, :] = per_volume * step
            ww[z, l, 8:24, :] = relative
            ww[z, l, 24:40, :] = through

    layers(0, NL, 2, fluxes)

    theirs = pl.ds(LX * (1 - core), LX)
    out_rows = pl.ds(pl.multiple_of(16 * core, 16), 16)
    keep_p = local(8, res_p.at[own0], out_p.at[:, out_rows, :])
    give_p = remote(18, 15, res_p.at[theirs], out_p.at[:, out_rows, :], partner)

    def restore(ref, first, count):
        at = pl.ds(first, count)
        value = ref[at].reshape(16 * count, 512)
        ref[at] = permuted(value, back[...], 3).reshape(count, 16, 512)

    def hand_back_pressure():
        for first in (0, 16):
            restore(res_p, first, 16)
        keep_p.start()
        give_p.start()

    pl.when(low)(hand_back_pressure)

    def newton(s, c, relative):
        q = s * s
        d = 1.5 * q + (0.5 - s)
        return d * d + relative * (s - q), d * (d * (s - c) + relative * q)

    waves, keeps, gives = [], [], []
    for half in (0, 1):
        tiles = (2 * half, 2 * half + 1)
        wide = pl.ds(256 * half, 256)
        waves.append(remote(19 + half, 16 + half, face_out.at[half], face_in.at[half], (gx + 2, gy)))
        keeps.append(local(10 + half, res_s.at[own0, :, wide], out_s.at[:, out_rows, wide]))
        gives.append(remote(21 + half, 18 + half, res_s.at[theirs, :, wide], out_s.at[:, out_rows, wide], partner))

        @pl.when(jnp.logical_not(low))
        def _(half=half, tiles=tiles):
            for z in tiles:
                face_in[half, z % 2] = st_b[0, :, lanes(z)]

        arrived(16 + half, face_in.at[half], low)

        def sweep(l, coming, tiles=tiles):
            going = []
            for z in tiles:
                relative = ww[z, l, 8:24, :]
                inflow = coming[z % 2]
                c = hh[z, l, 8:24, :] + hh[z, l, 24:40, :] * inflow
                s = jnp.clip(pb[z, l, 8:24, :] + pb[z, l, 24:40, :] * inflow, 0.0, 1.0)
                below, above = newton(s, c, relative)
                s = jnp.clip(s - above * recip(below), 0.0, 1.0)
                below, above = newton(s, c, relative)
                top = jnp.minimum(jnp.maximum(s * below - above, 0.0), below)
                res_s[l, :, lanes(z)] = top * recip(below)
                rest = (below - top) * (MOBILITY**0.5)
                top = top * top
                going.append(ww[z, l, 24:40, :] * top * recip(top + rest * rest))
            return going

        coming = lax.fori_loop(0, NL, sweep, [face_in[half, 0], face_in[half, 1]])
        for z in (0, 1):
            face_out[half, z] = coming[z]
        pl.when(high)(waves[half].start)
        keeps[half].start()
        gives[half].start()

    pl.when(jnp.logical_not(low))(hand_back_pressure)

    for ok, copy in sends + sends_late:
        guarded(ok, copy.wait_send)
    keep_p.wait()
    give_p.wait()
    for half in (0, 1):
        keeps[half].wait()
        pl.when(high)(waves[half].wait_send)
        gives[half].wait()


def finish_kernel(p_in, s_in, p_out, s_out, held, back, sem):
    across = pltpu.make_async_copy(p_in, p_out, sem.at[0])
    across.start()
    parts = []
    for i in range(4):
        at = pl.ds(4 * i, 4)
        parts.append((
            pltpu.make_async_copy(s_in.at[at], held.at[at], sem.at[1 + i]),
            pltpu.make_async_copy(held.at[at], s_out.at[at], sem.at[5 + i]),
        ))
        parts[i][0].start()
    ahead = lax.broadcasted_iota(jnp.int32, (512, 512), 0)
    aside = lax.broadcasted_iota(jnp.int32, (512, 512), 1)
    back[...] = jnp.where(4 * lax.rem(ahead, 128) + ahead // 128 == aside, 1.0, 0.0).astype(jnp.bfloat16)
    for i in range(4):
        parts[i][0].wait()
        at = pl.ds(4 * i, 4)
        value = held[at].reshape(128, 512)
        held[at] = permuted(value, back[...], 3).reshape(4, 32, 512)
        parts[i][1].start()
    for i in range(4):
        parts[i][1].wait()
    across.wait()


def shards(rock, perm_tab, poro_tab, base, press, sat0, wells, well_rates):
    f32, i32 = jnp.float32, jnp.int32
    shape = jax.ShapeDtypeStruct(rock.shape, f32)
    hbm = pl.BlockSpec(memory_space=pl.ANY)
    smem = pl.BlockSpec(memory_space=pltpu.SMEM)
    vmem = pl.BlockSpec(memory_space=pltpu.VMEM)
    extended = pltpu.VMEM((4, EL, ER, 128), f32)
    block = pltpu.VMEM((LX, 32, 512), f32)
    halfway = pl.pallas_call(
        step_kernel,
        out_shape=(shape, shape),
        in_specs=[hbm, smem, smem, hbm, hbm, hbm, vmem, vmem],
        out_specs=(hbm, hbm),
        scratch_shapes=[
            pltpu.VMEM((EL, 24, 512), f32),
            pltpu.VMEM((EL, 24, 512), f32),
            pltpu.VMEM((NL, 24, 512), f32),
            pltpu.VMEM((NL, 16, 512), f32),
            pltpu.VMEM((LX, 32, 512), i32),
            block, block, block, block, block, block, block,
            pltpu.VMEM((2, 5, LX, 512), f32),
            pltpu.VMEM((2, 5, LX, 512), f32),
            pltpu.VMEM((2, LX, 512), f32),
            pltpu.VMEM((4, 2, 4, 16, 128), f32),
            pltpu.VMEM((5, NL, 512), f32),
            pltpu.VMEM((5, NL, 512), f32),
            pltpu.VMEM((NL, 512), f32),
            pltpu.VMEM((2, 2, 2, 4, 16, 128), f32),
            extended, extended, extended, extended, extended, extended, extended, extended, extended,
            pltpu.VMEM((4, EL + 1, 24, 128), f32),
            pltpu.VMEM((24 * (EL + 1), 2 * WELLS), jnp.bfloat16),
            pltpu.VMEM((512, 2 * WELLS), jnp.bfloat16),
            pltpu.VMEM((4, NL, 32, 128), f32),
            pltpu.VMEM((512, 512), jnp.bfloat16),
            pltpu.VMEM((512, 512), jnp.bfloat16),
            pltpu.VMEM((2, 2, 16, 128), f32),
            pltpu.VMEM((2, 2, 16, 128), f32),
            pltpu.VMEM((NL, 16, 512), f32),
            pltpu.VMEM((NL, 16, 512), f32),
            pltpu.SemaphoreType.DMA((12,)),
            pltpu.SemaphoreType.DMA((23,)),
            pltpu.SemaphoreType.DMA((20,)),
        ],
        compiler_params=pltpu.CompilerParams(
            collective_id=0, has_side_effects=True, vmem_limit_bytes=60 * 1024 * 1024
        ),
    )(rock, perm_tab, poro_tab, base, press, sat0, wells, well_rates.reshape(1, WELLS))
    return pl.pallas_call(
        finish_kernel,
        out_shape=(shape, shape),
        in_specs=[hbm, hbm],
        out_specs=(hbm, hbm),
        scratch_shapes=[block, pltpu.VMEM((512, 512), jnp.bfloat16), pltpu.SemaphoreType.DMA((9,))],
        compiler_params=pltpu.CompilerParams(vmem_limit_bytes=60 * 1024 * 1024),
    )(*halfway)


def solution(mesh):
    block = P("gx", "gy", None)
    return jax.shard_map(
        shards,
        mesh=mesh,
        in_specs=(block, P(), P(), block, block, block, P(), P()),
        out_specs=(block, block),
        check_vma=False,
    )
```

time: 499 us -> 80.9 us (0.16)
  waiting for transfers between devices: 298 us -> 0 us
  starting transfers between devices: 92.6 us -> 0 us
  other arithmetic: 83.7 us -> 0 us
  Pallas kernels: 0 us -> 80.1 us
  local copies, waits for them, and re-layouts: 20 us -> 0 us
    ppermute x33 -> x0, waiting for transfers between devices: 298 us -> none  [the longest x9 287 us: passed_along(): return lax.ppermute(value, axis, pairs)]
    ppermute x33 -> x0, starting transfers between devices: 92.6 us -> none  [the longest x12 54 us: padded(): lax.ppermute(lax.slice_in_dim(block, 0, width, axis=dim), axis, backward)]
    pallas_call x0 -> x2, Pallas kernels: none -> 80.1 us  [the longest x1 47.2 us: shards(): pl.pallas_call(step_kernel, out_shape=(shape, shape), in_specs=[hbm, smem...]
    dynamic_update_slice x16 -> x0, other arithmetic: 27.8 us -> none  [sweep(): lax.scan(advance, inflow, (volume, through, explicit, old_sat))]
    mul x17 -> x0, other arithmetic: 19.5 us -> none  [the longest x16 10.4 us: advance(): return (flux_row * fraction(water), water)]
    add x4 -> x0, other arithmetic: 16.5 us -> none  [jacobi(): return center + OMEGA * (source - storage * center - flow) / diagonal]
    slice x17 -> x0, local copies, waits for them, and re-layouts: 12 us -> none  [the longest x2 3.24 us: lookup(): result = jnp.where(rock_type == kind, table[kind], result)]
    select_n x3 -> x0, other arithmetic: 6.57 us -> none  [the longest x1 5.91 us: lookup(): result = jnp.where(rock_type == kind, table[kind], result)]
  transfers between devices with their start and end apart: 33 -> 0, of which waited for: 12 -> 0; matrix products, arithmetic and copies ran while one was open for 7% -> 0% of each run, Pallas kernels for 0% -> 0%
where the time goes in v1:
time: 80.9 us; the launch traced here: 80.8 us
  Pallas kernels  80.1 us (99%)
    pallas_call x1, Pallas kernels, shards(): pl.pallas_call(step_kernel, out_shape=(shape, shape), in_specs=[hbm, smem...  47.2 us
    pallas_call x1, Pallas kernels, shards(): pl.pallas_call(finish_kernel, out_shape=(shape, shape), in_specs=[hbm, hb...  32.9 us

profile of v1, /device:TPU:103, one launch (start us, length us, event | category | flops | bytes accessed | tf_op | source)
XLA Modules:
  0.0 80.8 jit_solution(6983979298915978210)
XLA Ops:
  0.6 47.2 %shard_map.95 = (f32[16,32,512]{2,1,0:T(8,128)}, f32[16,32,512]{2,1,0:T(8,128)}) custom-call(s32[16,32,512]{2,1,0:T(8,128)} %rock.1, f32[8]{0:T(128)} %perm_tab.1, f32[8]{0:T(128)} %poro_tab.1, f32[16,32,512]{2,1,0:T(8,128)} %base.1, f32[16,32,512]{2,1,0:T(8,128)} %press.1, f32[16,32,512]{2,1,0:T(8,128)} %sat0.1, s32[3,512]{1,0:T(4,128)} %wells.1, ...), custom_call_target="tpu_custom_call" | custom-call | tf_op jit(solution)/shard_map/pallas_call | solution.py:577
  47.8 32.9 %shard_map.96 = (f32[16,32,512]{2,1,0:T(8,128)}, f32[16,32,512]{2,1,0:T(8,128)}) custom-call(f32[16,32,512]{2,1,0:T(8,128)} %get-tuple-element.4.p_in, f32[16,32,512]{2,1,0:T(8,128)} %get-tuple-element.5.s_in), custom_call_target="tpu_custom_call" | custom-call | tf_op jit(solution)/shard_map/pallas_call | solution.py:616

commit v2 on v1

--- a/solution.py
+++ b/solution.py
@@ -541,17 +541,21 @@
         gives[half].wait()
 
 
-def finish_kernel(p_in, s_in, p_out, s_out, held, back, sem):
-    across = pltpu.make_async_copy(p_in, p_out, sem.at[0])
-    across.start()
-    parts = []
+def finish_kernel(p_in, s_in, p_out, s_out, held_p, held, back, sem):
+    parts, plain = [], []
     for i in range(4):
         at = pl.ds(4 * i, 4)
         parts.append((
-            pltpu.make_async_copy(s_in.at[at], held.at[at], sem.at[1 + i]),
-            pltpu.make_async_copy(held.at[at], s_out.at[at], sem.at[5 + i]),
+            pltpu.make_async_copy(s_in.at[at], held.at[at], sem.at[i]),
+            pltpu.make_async_copy(held.at[at], s_out.at[at], sem.at[4 + i]),
+        ))
+        plain.append((
+            pltpu.make_async_copy(p_in.at[at], held_p.at[at], sem.at[8 + i]),
+            pltpu.make_async_copy(held_p.at[at], p_out.at[at], sem.at[12 + i]),
         ))
         parts[i][0].start()
+    for i in range(4):
+        plain[i][0].start()
     ahead = lax.broadcasted_iota(jnp.int32, (512, 512), 0)
     aside = lax.broadcasted_iota(jnp.int32, (512, 512), 1)
     back[...] = jnp.where(4 * lax.rem(ahead, 128) + ahead // 128 == aside, 1.0, 0.0).astype(jnp.bfloat16)
@@ -561,9 +565,11 @@
         value = held[at].reshape(128, 512)
         held[at] = permuted(value, back[...], 3).reshape(4, 32, 512)
         parts[i][1].start()
+        plain[i][0].wait()
+        plain[i][1].start()
     for i in range(4):
         parts[i][1].wait()
-    across.wait()
+        plain[i][1].wait()
 
 
 def shards(rock, perm_tab, poro_tab, base, press, sat0, wells, well_rates):
@@ -618,7 +624,7 @@
         out_shape=(shape, shape),
         in_specs=[hbm, hbm],
         out_specs=(hbm, hbm),
-        scratch_shapes=[block, pltpu.VMEM((512, 512), jnp.bfloat16), pltpu.SemaphoreType.DMA((9,))],
+        scratch_shapes=[block, block, pltpu.VMEM((512, 512), jnp.bfloat16), pltpu.SemaphoreType.DMA((16,))],
         compiler_params=pltpu.CompilerParams(vmem_limit_bytes=60 * 1024 * 1024),
     )(*halfway)
 

time: 80.9 us -> 51.4 us (0.64)
  Pallas kernels: 80.1 us -> 50.6 us
    pallas_call x1, Pallas kernels: 32.9 us -> 3.39 us  [shards(): pl.pallas_call(finish_kernel, out_shape=(shape, shape), in_specs=[hbm, hb...]
where the time goes in v2:
time: 51.4 us; the launch traced here: 51.2 us
  Pallas kernels  50.6 us (98%)
  between operations  0.64 us (1%)
    pallas_call x1, Pallas kernels, shards(): pl.pallas_call(step_kernel, out_shape=(shape, shape), in_specs=[hbm, smem...  47.2 us
    pallas_call x1, Pallas kernels, shards(): pl.pallas_call(finish_kernel, out_shape=(shape, shape), in_specs=[hbm, hb...  3.39 us

profile of v2, /device:TPU:103, one launch (start us, length us, event | category | flops | bytes accessed | tf_op | source)
XLA Modules:
  0.0 51.2 jit_solution(11872253034500311416)
XLA Ops:
  0.6 47.2 %shard_map.95 = (f32[16,32,512]{2,1,0:T(8,128)}, f32[16,32,512]{2,1,0:T(8,128)}) custom-call(s32[16,32,512]{2,1,0:T(8,128)} %rock.1, f32[8]{0:T(128)} %perm_tab.1, f32[8]{0:T(128)} %poro_tab.1, f32[16,32,512]{2,1,0:T(8,128)} %base.1, f32[16,32,512]{2,1,0:T(8,128)} %press.1, f32[16,32,512]{2,1,0:T(8,128)} %sat0.1, s32[3,512]{1,0:T(4,128)} %wells.1, ...), custom_call_target="tpu_custom_call" | custom-call | tf_op jit(solution)/shard_map/pallas_call | solution.py:583
  47.8 3.4 %shard_map.96 = (f32[16,32,512]{2,1,0:T(8,128)}, f32[16,32,512]{2,1,0:T(8,128)}) custom-call(f32[16,32,512]{2,1,0:T(8,128)} %get-tuple-element.4.p_in, f32[16,32,512]{2,1,0:T(8,128)} %get-tuple-element.5.s_in), custom_call_target="tpu_custom_call" | custom-call | tf_op jit(solution)/shard_map/pallas_call | solution.py:622

commit v3 on v2

--- a/solution.py
+++ b/solution.py
@@ -76,7 +76,7 @@
     out_p, out_s,
     st_r, st_p, st_s, st_b,
     in_r, in_p, in_s, in_b, my_r, my_p, my_s, my_b, pk_r, pk_p, pk_s, pk_c, ys_r, ys_p, ys_s, co,
-    hh, st, pa, pb, te, tn, tb, ww, src, rt, hot_a, hot_b, fs, order, back,
+    hh, st, pa, pb, pc, te, tn, tb, ww, src, rt, hot_a, hot_b, fs, order, back,
     face_in, face_out, res_p, res_s,
     loc, snd, rcv,
 ):
@@ -88,20 +88,27 @@
     f32 = jnp.float32
 
     barrier = pltpu.get_barrier_semaphore()
-    count = jnp.int32(0)
-    for dx in (-1, 0, 1):
-        for dy in (-1, 0, 1):
-            for other in (0, 1):
-                there = (xc + dx >= 0) & (xc + dx < NXC) & (gy + dy >= 0) & (gy + dy < NGY)
-                if dx == 0 and dy == 0:
-                    there = there & (core != other)
-                count = count + there.astype(jnp.int32)
-
-                @pl.when(there)
-                def _(dx=dx, dy=dy, other=other):
-                    pl.semaphore_signal(
-                        barrier, inc=1, device_id=(2 * (xc + dx) + other, gy + dy), device_id_type=MESH
-                    )
+    outer = ((core == 0) & down) | ((core == 1) & up)
+    outer_y = gy - 1 + 2 * core
+
+    def greet(ok, device):
+        def signal():
+            pl.semaphore_signal(barrier, inc=1, device_id=device, device_id_type=MESH)
+
+        signal() if ok is None else pl.when(ok)(signal)
+
+    greet(None, partner)
+    greet(low, (2 * xc - 1, gy))
+    greet(high, (2 * xc + 2, gy))
+    greet(low & (core == 0), (2 * xc - 2, gy))
+    greet(outer, (2 * xc, outer_y))
+    greet(outer, (2 * xc + 1, outer_y))
+    greet(outer & low, (2 * xc - 1, outer_y))
+    greet(outer & high, (2 * xc + 2, outer_y))
+    one = lambda ok: ok.astype(jnp.int32)
+    beside = jnp.where(core == 0, one(low), one(high))
+    across = one(down) + one(up)
+    count = 1 + 2 * beside + one(high & (core == 0)) + across * (1 + beside)
 
     def local(k, a, b):
         return pltpu.make_async_copy(a, b, loc.at[k])
@@ -317,6 +324,51 @@
     arrived(1, st_p.at[pl.ds(LO, LX)])
     by_core(lambda c: unpack_layers(LO, LO + NL, RO - 8 * c))
 
+    def side_faces(l, e0=8, e1=32, n0=0, n1=32):
+        for z in range(4):
+            te[z, l, e0:e1, :] = recip(hh[z, l, e0:e1, :] + hh[z, l + 1, e0:e1, :])
+            tn[z, l, n0:n1, :] = recip(hh[z, l, n0:n1, :] + hh[z, l, n0 + 1 : n1 + 1, :])
+
+    def weights(l, e0=8, e1=32):
+        own_h = [hh[z, l, e0:e1, :] for z in range(4)]
+        deeper = next_z(own_h)
+        below = [recip(own_h[z] + deeper[z]) for z in range(4)]
+        last = lax.broadcasted_iota(jnp.int32, (e1 - e0, 128), 1) == 127
+        below[3] = jnp.where(last, 0.0, below[3])
+        above = prev_z(below)
+        for z in (1, 2, 3, 0):
+            tb[z, l, e0:e1, :] = below[z]
+            storage = st[z, l, e0:e1, :]
+            diagonal = (
+                storage + te[z, l, e0:e1, :] + te[z, l - 1, e0:e1, :]
+                + tn[z, l, e0:e1, :] + tn[z, l, e0 - 1 : e1 - 1, :] + below[z] + above[z]
+            )
+            ww[z, l, e0:e1, :] = OMEGA * recip(diagonal)
+            src[z, l, e0:e1, :] = storage * pa[z, l, e0:e1, :] + rt[z, l, e0 - 8 : e1 - 8, :]
+
+    def one_pass(old, new, start, stop, block, e0=8, e1=32):
+        def body(l):
+            here = [old[z, l, e0:e1, :] for z in range(4)]
+            faces = [tb[z, l, e0:e1, :] for z in range(4)]
+            deeper = next_z(here)
+            shallower = prev_z([faces[z] * here[z] for z in range(4)])
+            for z in (1, 2, 3, 0):
+                total = (
+                    src[z, l, e0:e1, :] + faces[z] * deeper[z] + shallower[z]
+                    + te[z, l, e0:e1, :] * old[z, l + 1, e0:e1, :]
+                    + te[z, l - 1, e0:e1, :] * old[z, l - 1, e0:e1, :]
+                    + tn[z, l, e0:e1, :] * old[z, l, e0 + 1 : e1 + 1, :]
+                    + tn[z, l, e0 - 1 : e1 - 1, :] * old[z, l, e0 - 1 : e1 - 1, :]
+                )
+                new[z, l, e0:e1, :] = (1.0 - OMEGA) * here[z] + ww[z, l, e0:e1, :] * total
+
+        layers(start, stop, block, body)
+
+    layers(LO, LO + NL - 1, 4, side_faces)
+    layers(5, 35, 3, weights)
+    one_pass(pa, pb, 5, 35, 3)
+    one_pass(pb, pc, 6, 34, 4)
+
     def fraction(s):
         q = s * s
         return q * recip(1.5 * q + (0.5 - s))
@@ -375,60 +427,29 @@
 
     by_core(unpack_halo)
 
-    lane = lax.broadcasted_iota(jnp.int32, (24, 128), 1)
-    last = lane == 127
-
-    def side_faces(l):
-        for z in range(4):
-            te[z, l, 8:32, :] = recip(hh[z, l, 8:32, :] + hh[z, l + 1, 8:32, :])
-            tn[z, l, 0:32, :] = recip(hh[z, l, 0:32, :] + hh[z, l, 1:33, :])
-
-    layers(0, EL - 1, 2, side_faces)
-
-    def weights(l):
-        own_h = [hh[z, l, 8:32, :] for z in range(4)]
-        deeper = next_z(own_h)
-        below = [recip(own_h[z] + deeper[z]) for z in range(4)]
-        below[3] = jnp.where(last, 0.0, below[3])
-        above = prev_z(below)
-        for z in (1, 2, 3, 0):
-            tb[z, l, 8:32, :] = below[z]
-            storage = st[z, l, 8:32, :]
-            diagonal = (
-                storage + te[z, l, 8:32, :] + te[z, l - 1, 8:32, :]
-                + tn[z, l, 8:32, :] + tn[z, l, 7:31, :] + below[z] + above[z]
-            )
-            ww[z, l, 8:32, :] = OMEGA * recip(diagonal)
-            src[z, l, 8:32, :] = storage * pa[z, l, 8:32, :] + rt[z, l]
-
-    layers(1, EL - 1, 3, weights)
-
-    def one_pass(old, new, start, stop):
-        def body(l):
-            here = [old[z, l, 8:32, :] for z in range(4)]
-            faces = [tb[z, l, 8:32, :] for z in range(4)]
-            deeper = next_z(here)
-            shallower = prev_z([faces[z] * here[z] for z in range(4)])
-            for z in (1, 2, 3, 0):
-                total = (
-                    src[z, l, 8:32, :] + faces[z] * deeper[z] + shallower[z]
-                    + te[z, l, 8:32, :] * old[z, l + 1, 8:32, :]
-                    + te[z, l - 1, 8:32, :] * old[z, l - 1, 8:32, :]
-                    + tn[z, l, 8:32, :] * old[z, l, 9:33, :]
-                    + tn[z, l, 7:31, :] * old[z, l, 7:31, :]
-                )
-                new[z, l, 8:32, :] = (1.0 - OMEGA) * here[z] + ww[z, l, 8:32, :] * total
-
-        layers(start, stop, 3, body)
-
-    one_pass(pa, pb, 1, 40)
-    one_pass(pb, pa, 2, 39)
-    one_pass(pa, pb, 3, 38)
-    one_pass(pb, pa, 4, 37)
+    def finish_passes(c):
+        e0, e1 = (8, 16) if c == 0 else (24, 32)
+        n0 = 0 if c == 0 else 24
+        layers(0, LO, 2, side_faces)
+        layers(LO + NL - 1, EL - 1, 2, side_faces)
+        layers(LO, LO + NL - 1, 4, lambda l: side_faces(l, e0, e1, n0, e1))
+        layers(1, 5, 4, weights)
+        layers(35, 40, 5, weights)
+        layers(5, 35, 6, lambda l: weights(l, e0, e1))
+        one_pass(pa, pb, 1, 5, 4)
+        one_pass(pa, pb, 35, 40, 5)
+        one_pass(pa, pb, 5, 35, 6, e0, e1)
+        one_pass(pb, pc, 2, 6, 4)
+        one_pass(pb, pc, 34, 39, 5)
+        one_pass(pb, pc, 6, 34, 7, e0, e1)
+
+    by_core(finish_passes)
+    one_pass(pc, pa, 3, 38, 4)
+    one_pass(pa, pb, 4, 37, 4)
 
     def fluxes(l):
         e = l + LO
-        center = [pa[z, e, RO : RO + 16, :] for z in range(4)]
+        center = [pb[z, e, RO : RO + 16, :] for z in range(4)]
         frac = [fs[z, l, 8:24, :] for z in range(4)]
         deeper, frac_deep = next_z(center), next_z(frac)
         drained = []
@@ -441,10 +462,10 @@
             p, f = center[z], frac[z]
             res_p[l, :, lanes(z)] = p
             through = jnp.maximum(
-                st_b[l, :, lanes(z)] + te[z, e, RO : RO + 16, :] * (p - pa[z, e + 1, RO : RO + 16, :]), 0.0
+                st_b[l, :, lanes(z)] + te[z, e, RO : RO + 16, :] * (p - pb[z, e + 1, RO : RO + 16, :]), 0.0
             )
-            north = tn[z, e, RO : RO + 16, :] * (p - pa[z, e, RO + 1 : RO + 17, :])
-            south = tn[z, e, RO - 1 : RO + 15, :] * (p - pa[z, e, RO - 1 : RO + 15, :])
+            north = tn[z, e, RO : RO + 16, :] * (p - pb[z, e, RO + 1 : RO + 17, :])
+            south = tn[z, e, RO - 1 : RO + 15, :] * (p - pb[z, e, RO - 1 : RO + 15, :])
             leaving = drained[z] - entered[z]
             leaving = leaving + north * jnp.where(north > 0, f, fs[z, l, 9:25, :])
             leaving = leaving + south * jnp.where(south > 0, f, fs[z, l, 7:23, :])
@@ -460,8 +481,8 @@
             step = recip(1.0 + relative * slope)
             hh[z, l, 8:24, :] = s + extra
             hh[z, l, 24:40, :] = per_volume
-            pb[z, l, 8:24, :] = s + (extra - relative * f) * step
-            pb[z, l, 24:40, :] = per_volume * step
+            pc[z, l, 8:24, :] = s + (extra - relative * f) * step
+            pc[z, l, 24:40, :] = per_volume * step
             ww[z, l, 8:24, :] = relative
             ww[z, l, 24:40, :] = through
 
@@ -511,7 +532,7 @@
                 relative = ww[z, l, 8:24, :]
                 inflow = coming[z % 2]
                 c = hh[z, l, 8:24, :] + hh[z, l, 24:40, :] * inflow
-                s = jnp.clip(pb[z, l, 8:24, :] + pb[z, l, 24:40, :] * inflow, 0.0, 1.0)
+                s = jnp.clip(pc[z, l, 8:24, :] + pc[z, l, 24:40, :] * inflow, 0.0, 1.0)
                 below, above = newton(s, c, relative)
                 s = jnp.clip(s - above * recip(below), 0.0, 1.0)
                 below, above = newton(s, c, relative)
@@ -522,7 +543,7 @@
                 going.append(ww[z, l, 24:40, :] * top * recip(top + rest * rest))
             return going
 
-        coming = lax.fori_loop(0, NL, sweep, [face_in[half, 0], face_in[half, 1]])
+        coming = lax.fori_loop(0, NL, sweep, [face_in[half, 0], face_in[half, 1]], unroll=4)
         for z in (0, 1):
             face_out[half, z] = coming[z]
         pl.when(high)(waves[half].start)
@@ -600,7 +621,7 @@
             pltpu.VMEM((5, NL, 512), f32),
             pltpu.VMEM((NL, 512), f32),
             pltpu.VMEM((2, 2, 2, 4, 16, 128), f32),
-            extended, extended, extended, extended, extended, extended, extended, extended, extended,
+            extended, extended, extended, extended, extended, extended, extended, extended, extended, extended,
             pltpu.VMEM((4, EL + 1, 24, 128), f32),
             pltpu.VMEM((24 * (EL + 1), 2 * WELLS), jnp.bfloat16),
             pltpu.VMEM((512, 2 * WELLS), jnp.bfloat16),

time: 51.4 us -> 47.6 us (0.926)
  Pallas kernels: 50.6 us -> 46.8 us
    pallas_call x1, Pallas kernels: 47.2 us -> 43.3 us  [shards(): pl.pallas_call(step_kernel, out_shape=(shape, shape), in_specs=[hbm, smem...]
where the time goes in v3:
time: 47.6 us; the launch traced here: 47.4 us
  Pallas kernels  46.8 us (98%)
  between operations  0.64 us (1%)
    pallas_call x1, Pallas kernels, shards(): pl.pallas_call(step_kernel, out_shape=(shape, shape), in_specs=[hbm, smem...  43.3 us
    pallas_call x1, Pallas kernels, shards(): pl.pallas_call(finish_kernel, out_shape=(shape, shape), in_specs=[hbm, hb...  3.42 us

profile of v3, /device:TPU:103, one launch (start us, length us, event | category | flops | bytes accessed | tf_op | source)
XLA Modules:
  0.0 47.4 jit_solution(11342371055288972559)
XLA Ops:
  0.6 43.3 %shard_map.95 = (f32[16,32,512]{2,1,0:T(8,128)}, f32[16,32,512]{2,1,0:T(8,128)}) custom-call(s32[16,32,512]{2,1,0:T(8,128)} %rock.1, f32[8]{0:T(128)} %perm_tab.1, f32[8]{0:T(128)} %poro_tab.1, f32[16,32,512]{2,1,0:T(8,128)} %base.1, f32[16,32,512]{2,1,0:T(8,128)} %press.1, f32[16,32,512]{2,1,0:T(8,128)} %sat0.1, s32[3,512]{1,0:T(4,128)} %wells.1, ...), custom_call_target="tpu_custom_call" | custom-call | tf_op jit(solution)/shard_map/pallas_call | solution.py:604
  44.0 3.4 %shard_map.96 = (f32[16,32,512]{2,1,0:T(8,128)}, f32[16,32,512]{2,1,0:T(8,128)}) custom-call(f32[16,32,512]{2,1,0:T(8,128)} %get-tuple-element.4.p_in, f32[16,32,512]{2,1,0:T(8,128)} %get-tuple-element.5.s_in), custom_call_target="tpu_custom_call" | custom-call | tf_op jit(solution)/shard_map/pallas_call | solution.py:643

commit v4 on v3

--- a/solution.py
+++ b/solution.py
@@ -75,8 +75,8 @@
     rock, perm_tab, poro_tab, base, press, sat0, wells, well_rates,
     out_p, out_s,
     st_r, st_p, st_s, st_b,
-    in_r, in_p, in_s, in_b, my_r, my_p, my_s, my_b, pk_r, pk_p, pk_s, pk_c, ys_r, ys_p, ys_s, co,
-    hh, st, pa, pb, pc, te, tn, tb, ww, src, rt, hot_a, hot_b, fs, order, back,
+    in_r, my_r, my_p, my_s, my_b, pk_r, pk_p, pk_s, pk_c, ys_r, ys_p, ys_s, co,
+    hh, st, pa, pb, pc, pd, te, tn, tb, ww, src, rt, hot_a, hot_b, fs, order, back,
     face_in, face_out, res_p, res_s,
     loc, snd, rcv,
 ):
@@ -118,7 +118,7 @@
     own = pl.ds(LO + LX * core, LX)
     own0 = pl.ds(LX * core, LX)
     loads = [
-        local(0, rock, in_r), local(1, press, in_p), local(2, sat0, in_s), local(3, base, in_b)
+        local(0, rock, in_r), local(1, press, my_p), local(2, sat0, my_s), local(3, base, my_b)
     ]
     for copy in loads:
         copy.start()
@@ -194,7 +194,7 @@
     loads[0].wait()
     reorder(in_r, my_r, 1)
     loads[1].wait()
-    reorder(in_p, my_p, 3)
+    reorder(my_p, my_p, 3)
     for side in (0, 1):
         for a, b in ((my_r, pk_r), (my_p, pk_p)):
             for r in range(5):
@@ -219,11 +219,11 @@
     for ok, copy in sends:
         guarded(ok, copy.start)
     loads[2].wait()
-    reorder(in_s, my_s, 3)
+    reorder(my_s, my_s, 3)
     for side in (0, 1):
         pk_s[side] = my_s[:, 31 * side, :]
     loads[3].wait()
-    reorder(in_b, my_b, 3)
+    reorder(my_b, my_b, 3)
     blocks[2].start()
     blocks[3].start()
     for ok, copy in sends_late:
@@ -298,11 +298,14 @@
     tab_s = table(poro_tab, lambda v: (COMPRESS * VOLUME) * v) + [jnp.full((8, 128), 1.0, f32)]
 
     def lookup(kinds, n=8):
-        h, s = tab_h[0][:n], tab_s[0][:n]
+        def tall(value):
+            return value if n == 8 else jnp.concatenate([value] * (n // 8), axis=0)
+
+        h, s = tall(tab_h[0]), tall(tab_s[0])
         for k in range(1, ROCKS + 1):
             later = kinds > k - 0.5
-            h = jnp.where(later, tab_h[k][:n], h)
-            s = jnp.where(later, tab_s[k][:n], s)
+            h = jnp.where(later, tall(tab_h[k]), h)
+            s = jnp.where(later, tall(tab_s[k]), s)
         return h, s
 
     def unpack_layers(first, last, at_row, tiles=(0, 1, 2)):
@@ -388,24 +391,24 @@
 
     by_core(unpack_fraction)
 
-    arrived(4, ys_r, outer)
-    arrived(5, ys_p, outer)
-    arrived(6, ys_s, outer)
-    rows_here = pl.ds(pl.multiple_of(8 * core, 8), 16)
-    arrived(7, st_r.at[pl.ds(0, 4), rows_here, :], low)
-    arrived(8, st_p.at[pl.ds(0, 4), rows_here, :], low)
-    arrived(9, st_r.at[pl.ds(LO + NL, 5), rows_here, :], high)
-    arrived(10, st_p.at[pl.ds(LO + NL, 5), rows_here, :], high)
-    arrived(11, co.at[0, 0], low & outer)
-    arrived(12, co.at[0, 1], high & outer)
-    arrived(13, co.at[1, 0], low)
-    arrived(14, co.at[1, 1], high)
-
-    def unpack_halo(c):
+    def unpack_corner(kind, c):
+        e4 = 8 if c == kind else 28
+        for side, place in ((0, 0), (1, LO + NL)):
+            at = pl.ds(place, 4)
+            for r in range(4):
+                h, s = lookup(co[kind, side, 0, r], 16)
+                for z in range(4):
+                    hh[z, at, e4 + r, :] = h[4 * z : 4 * z + 4]
+                    st[z, at, e4 + r, :] = s[4 * z : 4 * z + 4]
+                    pa[z, at, e4 + r, :] = co[kind, side, 1, r, 4 * z : 4 * z + 4, :]
+
+    def unpack_along(c):
         unpack_layers(0, LO, RO - 8 * c, (c, c + 1))
         unpack_layers(LO + NL, EL, RO - 8 * c, (c, c + 1))
+        unpack_corner(1, c)
+
+    def unpack_across(c):
         e = 7 if c == 0 else 28
-
         for z in range(4):
             for r in range(5):
                 for g in range(4):
@@ -414,18 +417,23 @@
                     hh[z, at, e + r, :] = h
                     st[z, at, e + r, :] = s
                     pa[z, at, e + r, :] = ys_p[r, 8 * g : 8 * g + 8, lanes(z)]
-            for kind in (0, 1):
-                e4 = 8 if c == kind else 28
-                for r in range(4):
-                    for side, place in ((0, 0), (1, LO + NL)):
-                        at = pl.ds(place, 4)
-                        h, s = lookup(co[kind, side, 0, r, 4 * z : 4 * z + 4, :], 4)
-                        hh[z, at, e4 + r, :] = h
-                        st[z, at, e4 + r, :] = s
-                        pa[z, at, e4 + r, :] = co[kind, side, 1, r, 4 * z : 4 * z + 4, :]
             fs[z, :, 7 if c == 0 else 24, :] = fraction(ys_s[:, lanes(z)])
-
-    by_core(unpack_halo)
+        unpack_corner(0, c)
+
+    rows_here = pl.ds(pl.multiple_of(8 * core, 8), 16)
+    arrived(7, st_r.at[pl.ds(0, 4), rows_here, :], low)
+    arrived(8, st_p.at[pl.ds(0, 4), rows_here, :], low)
+    arrived(9, st_r.at[pl.ds(LO + NL, 5), rows_here, :], high)
+    arrived(10, st_p.at[pl.ds(LO + NL, 5), rows_here, :], high)
+    arrived(13, co.at[1, 0], low)
+    arrived(14, co.at[1, 1], high)
+    by_core(unpack_along)
+    arrived(4, ys_r, outer)
+    arrived(5, ys_p, outer)
+    arrived(6, ys_s, outer)
+    arrived(11, co.at[0, 0], low & outer)
+    arrived(12, co.at[0, 1], high & outer)
+    by_core(unpack_across)
 
     def finish_passes(c):
         e0, e1 = (8, 16) if c == 0 else (24, 32)
@@ -444,12 +452,12 @@
         one_pass(pb, pc, 6, 34, 7, e0, e1)
 
     by_core(finish_passes)
-    one_pass(pc, pa, 3, 38, 4)
-    one_pass(pa, pb, 4, 37, 4)
+    one_pass(pc, pd, 3, 38, 4)
+    one_pass(pd, pa, 4, 37, 4)
 
     def fluxes(l):
         e = l + LO
-        center = [pb[z, e, RO : RO + 16, :] for z in range(4)]
+        center = [pa[z, e, RO : RO + 16, :] for z in range(4)]
         frac = [fs[z, l, 8:24, :] for z in range(4)]
         deeper, frac_deep = next_z(center), next_z(frac)
         drained = []
@@ -462,10 +470,10 @@
             p, f = center[z], frac[z]
             res_p[l, :, lanes(z)] = p
             through = jnp.maximum(
-                st_b[l, :, lanes(z)] + te[z, e, RO : RO + 16, :] * (p - pb[z, e + 1, RO : RO + 16, :]), 0.0
+                st_b[l, :, lanes(z)] + te[z, e, RO : RO + 16, :] * (p - pa[z, e + 1, RO : RO + 16, :]), 0.0
             )
-            north = tn[z, e, RO : RO + 16, :] * (p - pb[z, e, RO + 1 : RO + 17, :])
-            south = tn[z, e, RO - 1 : RO + 15, :] * (p - pb[z, e, RO - 1 : RO + 15, :])
+            north = tn[z, e, RO : RO + 16, :] * (p - pa[z, e, RO + 1 : RO + 17, :])
+            south = tn[z, e, RO - 1 : RO + 15, :] * (p - pa[z, e, RO - 1 : RO + 15, :])
             leaving = drained[z] - entered[z]
             leaving = leaving + north * jnp.where(north > 0, f, fs[z, l, 9:25, :])
             leaving = leaving + south * jnp.where(south > 0, f, fs[z, l, 7:23, :])
@@ -612,7 +620,7 @@
             pltpu.VMEM((NL, 24, 512), f32),
             pltpu.VMEM((NL, 16, 512), f32),
             pltpu.VMEM((LX, 32, 512), i32),
-            block, block, block, block, block, block, block,
+            block, block, block, block,
             pltpu.VMEM((2, 5, LX, 512), f32),
             pltpu.VMEM((2, 5, LX, 512), f32),
             pltpu.VMEM((2, LX, 512), f32),
@@ -621,7 +629,8 @@
             pltpu.VMEM((5, NL, 512), f32),
             pltpu.VMEM((NL, 512), f32),
             pltpu.VMEM((2, 2, 2, 4, 16, 128), f32),
-            extended, extended, extended, extended, extended, extended, extended, extended, extended, extended,
+            extended, extended, extended, extended, extended, extended,
+            extended, extended, extended, extended, extended,
             pltpu.VMEM((4, EL + 1, 24, 128), f32),
             pltpu.VMEM((24 * (EL + 1), 2 * WELLS), jnp.bfloat16),
             pltpu.VMEM((512, 2 * WELLS), jnp.bfloat16),
@@ -645,7 +654,7 @@
         out_shape=(shape, shape),
         in_specs=[hbm, hbm],
         out_specs=(hbm, hbm),
-        scratch_shapes=[block, block, pltpu.VMEM((512, 512), jnp.bfloat16), pltpu.SemaphoreType.DMA((16,))],
+        scratch_shapes=[block, block, pltpu.VMEM((512, 512), jnp.bfloat16), pltpu.SemaphoreType.DMA((32,))],
         compiler_params=pltpu.CompilerParams(vmem_limit_bytes=60 * 1024 * 1024),
     )(*halfway)
 

time: 47.6 us -> 47.1 us (0.989)
  Pallas kernels: 46.8 us -> 46.3 us
    pallas_call x1, Pallas kernels: 43.3 us -> 42.7 us  [shards(): pl.pallas_call(step_kernel, out_shape=(shape, shape), in_specs=[hbm, smem...]
where the time goes in v4:
time: 47.1 us; the launch traced here: 46.9 us
  Pallas kernels  46.3 us (98%)
  between operations  0.64 us (1%)
    pallas_call x1, Pallas kernels, shards(): pl.pallas_call(step_kernel, out_shape=(shape, shape), in_specs=[hbm, smem...  42.7 us
    pallas_call x1, Pallas kernels, shards(): pl.pallas_call(finish_kernel, out_shape=(shape, shape), in_specs=[hbm, hb...  3.55 us

profile of v4, /device:TPU:103, one launch (start us, length us, event | category | flops | bytes accessed | tf_op | source)
XLA Modules:
  0.0 46.9 jit_solution(17609589520435171922)
XLA Ops:
  0.6 42.7 %shard_map.95 = (f32[16,32,512]{2,1,0:T(8,128)}, f32[16,32,512]{2,1,0:T(8,128)}) custom-call(s32[16,32,512]{2,1,0:T(8,128)} %rock.1, f32[8]{0:T(128)} %perm_tab.1, f32[8]{0:T(128)} %poro_tab.1, f32[16,32,512]{2,1,0:T(8,128)} %base.1, f32[16,32,512]{2,1,0:T(8,128)} %press.1, f32[16,32,512]{2,1,0:T(8,128)} %sat0.1, s32[3,512]{1,0:T(4,128)} %wells.1, ...), custom_call_target="tpu_custom_call" | custom-call | tf_op jit(solution)/shard_map/pallas_call | solution.py:612
  43.4 3.6 %shard_map.96 = (f32[16,32,512]{2,1,0:T(8,128)}, f32[16,32,512]{2,1,0:T(8,128)}) custom-call(f32[16,32,512]{2,1,0:T(8,128)} %get-tuple-element.4.p_in, f32[16,32,512]{2,1,0:T(8,128)} %get-tuple-element.5.s_in), custom_call_target="tpu_custom_call" | custom-call | tf_op jit(solution)/shard_map/pallas_call | solution.py:652
